TPU v7x, 32 devices: a whole 2x2x4 slice. The times are simulated.
32 devices in a mesh: dom: 8 (over z, x), grp: 4 (over y, core).
Axes of the slice: x: 2, y: 2, z: 4, core: 2. Of those that a mesh axis runs over, the one named last changes fastest.
Arguments:
- node_feats: bfloat16 [8192, 1024], P(('dom', 'grp')), may hold values from -6 to 6
- weight: bfloat16 [1024, 512], replicated, may hold values from -0.1875 to 0.1875
- bias: float32 [512], replicated, may hold values from -4 to 4
- cotangent: bfloat16 [8192, 512], P(('dom', 'grp')), may hold values from -6 to 6
- tile_bank: bfloat16 [16, 128, 128], replicated, may hold values from -0.125 to 0.125
- local_cols: int32 [8, 8, 16], P('dom'), may hold values from 0 to 7
- local_banks: int32 [8, 8, 16], P('dom'), may hold values from 0 to 15
- published: int32 [8, 4], P('dom'), may hold values from 0 to 7, as said below
- send_table: int32 [8, 8, 2], replicated, may hold values from -1 to 3, as said below
- halo_rows: int32 [8, 8, 2], P('dom'), may hold values from 0 to 7
- halo_banks: int32 [8, 8, 2], P('dom'), may hold values from 0 to 15
Outputs:
- activations: bfloat16 [8192, 512], P(('dom', 'grp'))
- grad_nodes: bfloat16 [8192, 1024], P(('dom', 'grp'))
- grad_weight: float32 [1024, 512], replicated
- grad_bias: float32 [512], replicated
Inputs may be any that keep to these rules, and one draw needn't show every extreme that they name: `published`: the 4 entries of a partition are distinct block numbers of that partition; 0 and 7 each appear in some partition's list. `send_table`: entry s of the pair (src, p) is -1 or an index into the offered list of src; the live entries of a pair come first and are distinct; a pair (p, p) has none; some pair has all 2 entries live.
All inputs are finite; a program needn't handle non-finite values.
Results may differ from a plain program's by a relative error of at most 0.019.
The roundings to bfloat16 on the way count: a program that leaves them out, or rounds other values in their place, can miss the bound.
Values may be sent and summed in bfloat16 or wider, within the bound.
No kernel may reach another device: no remote copies, remote signals or barrier semaphores. Data moves between devices by JAX's collectives and lax.ppermute only.
A program may use at most 64 MiB of HBM per device.

v0:
```python
import functools

import jax
import jax.numpy as jnp
from jax import lax
from jax.experimental import pallas as pl
from jax.experimental.pallas import tpu as pltpu
from jax.sharding import PartitionSpec as P

VMEM = pl.BlockSpec(memory_space=pltpu.VMEM)
SMEM = pl.BlockSpec(memory_space=pltpu.SMEM)
EXTRA = 16
COPIES = 4
F32 = jnp.float32
BF16 = jnp.bfloat16


def call(
    body, out_shape, specs, scratch=(), flops=0, nbytes=0, name=None, out_specs=None, aliases=(), mib=16
):
    return pl.pallas_call(
        body,
        out_shape=out_shape,
        in_specs=specs,
        out_specs=jax.tree.map(lambda _: VMEM, out_shape) if out_specs is None else out_specs,
        scratch_shapes=list(scratch),
        input_output_aliases=dict(aliases),
        compiler_params=pltpu.CompilerParams(vmem_limit_bytes=mib * 1024 * 1024),
        cost_estimate=pl.CostEstimate(flops=flops, bytes_accessed=nbytes, transcendentals=0),
        name=name,
    )


def shape(dims, kind):
    return jax.ShapeDtypeStruct(tuple(dims), kind)


def dot(a, b):
    return jnp.dot(a, b, preferred_element_type=F32)


def bias_rows(total):
    high = total.astype(BF16).astype(F32)
    rest = jnp.zeros((EXTRA - 2, total.shape[1]), F32)
    return jnp.concatenate([high, total - high, rest], axis=0).astype(BF16)


def aligned(start, step):
    return pl.ds(pl.multiple_of(start * step, step), step)


def swap(value, axis, mask):
    return lax.ppermute(value, axis, [(i, i ^ mask) for i in range(lax.axis_size(axis))])


def exchange(parts, axis):
    return list(parts[:1]) + [swap(part, axis, m) for m, part in enumerate(parts[1:], 1)]


def spread(value, axis, bit):
    parts, masks = [value], [0]
    while bit:
        parts = parts + [swap(part, axis, bit) for part in parts]
        masks = masks + [mask ^ bit for mask in masks]
        bit //= 2
    return parts, masks


def split_features(ids, feats, *refs):
    outs, sems = refs[:-1], refs[-1]
    group = ids[1]
    narrow = outs[0].shape[1]
    copies = [
        pltpu.make_async_copy(
            feats.at[:, aligned(jnp.bitwise_xor(group, m), narrow)], out, sems.at[m]
        )
        for m, out in enumerate(outs)
    ]
    for copy in copies:
        copy.start()
    for copy in copies:
        copy.wait()


def pick_blocks(groups, slots, at, tab, *refs):
    parts, (x, offered, *outs) = refs[:groups], refs[groups:]
    domain, group = tab[at["me"]], tab[at["me"] + 1]
    tile = x.shape[1]
    per = x.shape[0] // groups
    for m, part in zip(reversed(range(groups)), parts):
        owner = jnp.bitwise_xor(group, m)
        for j in range(per):
            x[owner * per + j] = part[j * tile : (j + 1) * tile]
    for j in range(offered.shape[0]):
        offered[j] = x[tab[at["pub"] + j]]
    for m, out in enumerate(outs, 1):
        reader = jnp.bitwise_xor(domain, m)
        for s in range(slots):
            entry = jnp.maximum(tab[at["out"] + reader * slots + s], 0)
            out[s * tile : (s + 1) * tile] = x[tab[at["pub"] + entry]]


def pick_relayed(slots, at, tab, offered, *outs):
    tile = offered.shape[1]
    for m, out in enumerate(outs, 1):
        reader = jnp.bitwise_xor(tab[at["me"]], m)
        for s in range(slots):
            entry = jnp.maximum(tab[at["out2"] + reader * slots + s], 0)
            out[s * tile : (s + 1) * tile] = offered[entry]


def local_sum(per_row, at, tab, bank, x, out):
    pair = 2 if per_row % 2 == 0 else 1

    @pl.loop(0, out.shape[0])
    def _(r):
        acc = jnp.zeros(out.shape[1:], F32)
        for k in range(0, per_row, pair):
            spots = [r * per_row + k + j for j in range(pair)]
            left = jnp.concatenate([bank[tab[at["banks"] + a]] for a in spots], axis=1)
            right = jnp.concatenate([x[tab[at["cols"] + a]] for a in spots], axis=0)
            acc += dot(left, right)
        out[r] = acc


def halo_adder(slots, at, tab, bank, acc):
    def add(source, get):
        for s in range(slots):
            i = source * slots + s
            entry = tab[at["in"] + i]

            @pl.when(entry >= 0)
            def _(i=i, s=s, entry=entry):
                acc[tab[at["hrows"] + i]] += dot(bank[tab[at["hbanks"] + i]], get(s, entry))

    return add


def add_near(slots, at, tab, bank, local, mirrored, *refs):
    near, acc = refs[:-1], refs[-1]
    domain = tab[at["me"]]
    tile = local.shape[1]
    acc[...] = local[...]
    add = halo_adder(slots, at, tab, bank, acc)
    for m, block in enumerate(near, 1):
        add(jnp.bitwise_xor(domain, m), lambda s, _, block=block: block[s * tile : (s + 1) * tile])
    mirror = jnp.bitwise_xor(domain, len(near) + 1)
    add(mirror, lambda _, entry: mirrored[jnp.maximum(entry, 0)])


def add_far(half, groups, slots, at, tab, bank, local, *refs):
    far, outs, acc = refs[: half - 1], refs[half - 1 : -1], refs[-1]
    domain, group = tab[at["me"]], tab[at["me"] + 1]
    tile = local.shape[1]
    per = local.shape[0] // groups
    acc[...] = local[...]
    add = halo_adder(slots, at, tab, bank, acc)
    for m, block in enumerate(far, half + 1):
        add(jnp.bitwise_xor(domain, m), lambda s, _, block=block: block[s * tile : (s + 1) * tile])
    for m, out in enumerate(outs):
        owner = jnp.bitwise_xor(group, m)
        for j in range(per):
            out[j * tile : (j + 1) * tile] = acc[owner * per + j].astype(BF16)


def dense(groups, ids, weight, bias, cot, *refs):
    parts, (act, grad, *slices) = refs[:groups], refs[groups:]
    group = ids[1]
    narrow = parts[0].shape[1]
    wide = cot.shape[1] // groups
    left = jnp.concatenate([part[...] for part in parts], axis=1)
    spots = [aligned(jnp.bitwise_xor(group, m), narrow) for m in range(groups)]
    pre = dot(left, jnp.concatenate([weight[spot] for spot in spots], axis=0)) + bias[...]
    act[...] = jnp.maximum(pre, 0.0).astype(BF16)
    masked = jnp.where(pre > 0, cot[...].astype(F32), 0.0).astype(BF16)
    for s in range(groups):
        grad[s] = masked[:, s * wide : (s + 1) * wide]
    for m, out in enumerate(slices):
        out[...] = grad[jnp.bitwise_xor(group, m)]


def write_out(value, out):
    out[...] = value[...]


def back_halo(groups, slots, at, tab, bank_t, *refs):
    parts, (own, mine, kept, *terms) = refs[:groups], refs[groups:]
    domain, group = tab[at["me"]], tab[at["me"] + 1]
    tile = bank_t.shape[1]
    per = parts[0].shape[0] // tile
    half = len(terms) + 1
    total = jnp.zeros((1, own.shape[2]), F32)
    for m, part in enumerate(parts):
        owner = jnp.bitwise_xor(group, m)
        piece = part[...]
        total += jnp.sum(piece.astype(F32), axis=0, keepdims=True)
        for j in range(per):
            own[owner * per + j] = piece[j * tile : (j + 1) * tile]
    mine[...] = total
    tail = bias_rows(total)

    def put(out, place, source):
        for s in range(slots):
            i = source * slots + s
            live = (tab[at["in"] + i] >= 0).astype(F32)
            value = dot(bank_t[tab[at["hbanks"] + i]], own[tab[at["hrows"] + i]]) * live
            spot = (place * slots + s) * tile
            out[spot : spot + tile] = value.astype(BF16)

    for m, term in enumerate(terms, 1):
        peer = jnp.bitwise_xor(domain, m)
        put(term, 0, peer)
        put(term, 1, jnp.bitwise_xor(peer, half))
        term[2 * slots * tile :] = tail
    put(kept, 0, jnp.bitwise_xor(domain, half))


def sum_mirror(slots, at, tab, mine, kept, *refs):
    recv, out, acc = refs[:-2], refs[-2], refs[-1]
    domain = tab[at["me"]]
    offered, tile = acc.shape[:2]
    acc[...] = jnp.zeros_like(acc)
    total = mine[...]
    for m, block in enumerate((kept,) + recv):
        reader = jnp.bitwise_xor(domain, m)
        for s in range(slots):
            entry = tab[at["out2"] + reader * slots + s]
            spot = (s + (slots if m else 0)) * tile

            @pl.when(entry >= 0)
            def _(entry=entry, spot=spot, block=block):
                acc[jnp.maximum(entry, 0)] += block[spot : spot + tile].astype(F32)

        if m:
            tail = block[2 * slots * tile :].astype(F32)
            total += tail[0:1] + tail[1:2]
    for j in range(offered):
        out[j * tile : (j + 1) * tile] = acc[j].astype(BF16)
    out[offered * tile :] = bias_rows(total)


def weight_part(groups, *refs):
    aggs, (grad, send, keep) = refs[:groups], refs[groups:]
    right = jnp.concatenate([grad[s] for s in range(groups)], axis=1)
    for m, agg in enumerate(aggs):
        value = lax.dot_general(
            agg[...], right, (((0,), (0,)), ((), ())), preferred_element_type=F32
        )
        out = send if m % 2 else keep
        out[m // 2] = value.astype(out.dtype)


def fold(kept, recv, send, keep):
    for j in range(kept.shape[0]):
        out = send if j % 2 else keep
        out[j // 2] = (kept[j] + recv[j].astype(F32)).astype(out.dtype)


def weight_shares(ids, whole, recv, *refs):
    kept, *outs = refs[:-1]
    total = refs[-1]
    domain = ids[0]
    half = len(outs) + 1
    rows = total.shape[1]
    value = whole[0] + recv[0].astype(F32)
    for d in range(total.shape[0]):
        total[d] = value[d * rows : (d + 1) * rows]
    for m, out in enumerate([kept] + outs):
        peer = jnp.bitwise_xor(domain, m)
        out[0] = total[peer].astype(out.dtype)
        out[1] = total[jnp.bitwise_xor(peer, half)].astype(out.dtype)


def sum_half(kept, *refs):
    recv, out = refs[:-1], refs[-1]
    for i in range(2):
        total = kept[i]
        for block in recv:
            total += block[i].astype(F32)
        out[i] = total.astype(BF16)


def sum_both(scale, here, there, out):
    for i in range(2):
        out[i] = ((here[i].astype(F32) + there[1 - i].astype(F32)) * scale).astype(BF16)


def join_shares(ids, *refs):
    parts, out = refs[:-1], refs[-1]
    for m, part in enumerate(parts):
        owner = jnp.bitwise_xor(ids[0], m)
        out[owner] = part[0]
        out[jnp.bitwise_xor(owner, len(parts))] = part[1]


def back_local(per_row, at, tab, bank_t, own, out):
    out[...] = jnp.zeros_like(out)

    @pl.loop(0, own.shape[0])
    def _(r):
        right = own[r]
        for k in range(per_row):
            spot = r * per_row + k
            out[tab[at["cols"] + spot]] += dot(bank_t[tab[at["banks"] + spot]], right)


def finish_nodes(half, slots, scale, at, tab, local, mine, mirrored, *refs):
    recv, outs, acc = refs[: half - 1], refs[half - 1 : -1], refs[-1]
    groups = len(outs)
    domain, group = tab[at["me"]], tab[at["me"] + 1]
    tile = local.shape[1]
    per = local.shape[0] // groups
    offered = (mirrored.shape[0] - EXTRA) // tile
    acc[...] = local[...]
    tail = mirrored[offered * tile :].astype(F32)
    for j in range(offered):
        acc[tab[at["pub"] + j]] += mirrored[j * tile : (j + 1) * tile].astype(F32)
    for m, block in enumerate(recv, 1):
        tail += block[2 * slots * tile :].astype(F32)
        reader = jnp.bitwise_xor(domain, m)
        for s in range(slots):
            entry = tab[at["out"] + reader * slots + s]

            @pl.when(entry >= 0)
            def _(s=s, entry=entry, block=block):
                spot = tab[at["pub"] + jnp.maximum(entry, 0)]
                acc[spot] += block[s * tile : (s + 1) * tile].astype(F32)

    rows = bias_rows((mine[...] + tail[0:1] + tail[1:2]) * scale)
    for m, out in enumerate(outs):
        owner = jnp.bitwise_xor(group, m)
        for j in range(per):
            out[j * tile : (j + 1) * tile] = acc[owner * per + j].astype(BF16)
        out[per * tile :] = rows


def node_grads(groups, ids, weight, *refs):
    parts, (out, bias_out, hid) = refs[:groups], refs[groups:]
    group = ids[1]
    rows = out.shape[0]
    for m, part in enumerate(parts):
        hid[jnp.bitwise_xor(group, m)] = part[...]
    left = jnp.concatenate([hid[s, :rows] for s in range(groups)], axis=1)
    out[...] = lax.dot_general(
        left, weight[...], (((1,), (1,)), ((), ())), preferred_element_type=F32
    ).astype(BF16)
    tail = jnp.concatenate([hid[s, rows:] for s in range(groups)], axis=1).astype(F32)
    bias_out[...] = tail[0:1] + tail[1:2]


def place_weight(masks, ids, *refs):
    parts, (out, wide, sems) = refs[: len(masks)], refs[-3:]
    group = ids[1]
    rows = parts[0].shape[0]
    copies = []
    step = rows // COPIES
    for i, (mask, part) in enumerate(zip(masks, parts)):
        for j in range(COPIES):
            wide[i, j * step : (j + 1) * step] = part[j * step : (j + 1) * step].astype(F32)
            spot = out.at[aligned(jnp.bitwise_xor(group, mask) * COPIES + j, step)]
            piece = wide.at[i, pl.ds(j * step, step)]
            copies.append(pltpu.make_async_copy(piece, spot, sems.at[i, j]))
            copies[-1].start()
    for copy in copies:
        copy.wait()


def per_device(
    node_feats,
    weight,
    bias,
    cotangent,
    tile_bank,
    local_cols,
    local_banks,
    published,
    send_table,
    halo_rows,
    halo_banks,
):
    domains = lax.axis_size("dom")
    groups = lax.axis_size("grp")
    domain_index = lax.axis_index("dom")
    rows_here, embed = node_feats.shape
    hidden = weight.shape[1]
    tile = tile_bank.shape[1]
    slots = send_table.shape[2]
    per_row = local_cols.shape[2]
    part_rows = rows_here * groups
    blocks = part_rows // tile
    narrow = embed // groups
    wide = hidden // groups
    share = narrow // domains
    half = domains // 2
    peers = half - 1
    offers = published.shape[1]

    ids = jnp.stack([domain_index, lax.axis_index("grp")]).astype(jnp.int32)
    tables = {
        "cols": local_cols[0],
        "banks": local_banks[0],
        "pub": published[0],
        "out": lax.dynamic_index_in_dim(send_table, domain_index, 0, keepdims=False),
        "out2": lax.dynamic_index_in_dim(send_table, domain_index ^ half, 0, keepdims=False),
        "in": lax.dynamic_index_in_dim(send_table, domain_index, 1, keepdims=False),
        "hrows": halo_rows[0],
        "hbanks": halo_banks[0],
        "me": ids,
    }
    at, place = {}, 0
    for name, table in tables.items():
        at[name] = place
        place += table.size
    tab = jnp.concatenate([table.reshape(-1) for table in tables.values()])
    bank_t = jnp.swapaxes(tile_bank, 1, 2)

    feats = call(
        split_features,
        [shape((rows_here, narrow), BF16)] * groups,
        [SMEM, pl.BlockSpec(memory_space=pl.ANY)],
        [pltpu.SemaphoreType.DMA((groups,))],
        nbytes=4 * rows_here * embed,
        name="split_features",
    )(ids, node_feats)
    feats = exchange(feats, "grp")
    x, offered, *picked = call(
        functools.partial(pick_blocks, groups, slots, at),
        [shape((blocks, tile, narrow), BF16), shape((offers, tile, narrow), BF16)]
        + [shape((slots * tile, narrow), BF16)] * peers,
        [SMEM] + [VMEM] * groups,
        nbytes=4 * (peers * slots + blocks + offers) * tile * narrow,
        name="pick_blocks",
    )(tab, *reversed(feats))
    mirrored = swap(offered, "dom", half)
    near = exchange([None] + picked, "dom")[1:]
    local = call(
        functools.partial(local_sum, per_row, at),
        shape((blocks, tile, narrow), F32),
        [SMEM, VMEM, VMEM],
        flops=2 * blocks * per_row * tile * tile * narrow,
        nbytes=blocks * tile * narrow * 6,
        name="local_sum",
    )(tab, tile_bank, x)
    mirrored, local = lax.optimization_barrier((mirrored, local))
    relayed = call(
        functools.partial(pick_relayed, slots, at),
        [shape((slots * tile, narrow), BF16)] * peers,
        [SMEM, VMEM],
        nbytes=4 * peers * slots * tile * narrow,
        name="pick_relayed",
    )(tab, mirrored)
    far = exchange([None, *relayed], "dom")[1:]
    local = call(
        functools.partial(add_near, slots, at),
        shape((blocks, tile, narrow), F32),
        [SMEM, VMEM, VMEM, VMEM] + [VMEM] * peers,
        flops=2 * half * slots * tile * tile * narrow,
        nbytes=blocks * tile * narrow * 8,
        name="add_near",
    )(tab, tile_bank, local, mirrored, *near)
    far, local = lax.optimization_barrier((far, local))
    aggs = call(
        functools.partial(add_far, half, groups, slots, at),
        [shape((rows_here, narrow), BF16)] * groups,
        [SMEM, VMEM, VMEM] + [VMEM] * peers,
        [pltpu.VMEM((blocks, tile, narrow), F32)],
        flops=2 * half * slots * tile * tile * narrow,
        nbytes=blocks * tile * narrow * 8,
        name="add_far",
    )(tab, tile_bank, local, *far)
    mine = exchange(aggs, "grp")
    activations, grad, *grads = call(
        functools.partial(dense, groups),
        [shape((rows_here, hidden), BF16), shape((groups, rows_here, wide), BF16)]
        + [shape((rows_here, wide), BF16)] * groups,
        [SMEM] + [VMEM] * (3 + groups),
        flops=2 * rows_here * embed * hidden,
        nbytes=embed * hidden * 2 + rows_here * (embed + 4 * hidden) * 2,
        name="dense",
    )(ids, weight, bias.reshape(1, hidden), cotangent, *mine)
    grads = exchange(grads, "grp")
    activations = call(
        write_out,
        shape((rows_here, hidden), BF16),
        [VMEM],
        nbytes=4 * rows_here * hidden,
        name="write_out",
    )(activations)
    norm_scale = float(rows_here * groups * domains) ** (-0.5)
    norm_scale = float(rows_here * groups * domains) ** (-0.5)
    send, keep = call(
        functools.partial(weight_part, groups),
        [
            shape((groups // 2, narrow, hidden), BF16),
            shape((groups // 2, narrow, hidden), F32),
        ],
        [VMEM] * (groups + 1),
        flops=2 * rows_here * embed * hidden,
        nbytes=rows_here * (embed + hidden) * 2 + embed * hidden * 3,
        name="weight_part",
    )(*mine, grad)
    recv = swap(send, "grp", 1)
    recv, grads, activations = lax.optimization_barrier((recv, grads, activations))
    bit = 2
    while bit < groups:
        count = groups // (2 * bit)
        send, keep = call(
            fold,
            [shape((count, narrow, hidden), BF16), shape((count, narrow, hidden), F32)],
            [VMEM, VMEM],
            nbytes=count * narrow * hidden * 18,
            name="fold",
        )(keep, recv)
        recv = swap(send, "grp", bit)
        bit *= 2
    tab_after, _ = lax.optimization_barrier((tab, send))
    own, bias_here, kept, *terms = call(
        functools.partial(back_halo, groups, slots, at),
        [
            shape((blocks, tile, wide), BF16),
            shape((1, wide), F32),
            shape((slots * tile, wide), BF16),
        ]
        + [shape((2 * slots * tile + EXTRA, wide), BF16)] * peers,
        [SMEM, VMEM] + [VMEM] * groups,
        flops=2 * domains * slots * tile * tile * wide,
        nbytes=(domains * slots + blocks) * tile * wide * 2,
        name="back_halo",
    )(tab_after, bank_t, *grads)
    terms = exchange([None] + terms, "dom")[1:]
    recv, terms[0] = lax.optimization_barrier((recv, terms[0]))
    kept_shares, *shares = call(
        weight_shares,
        [shape((2, share, hidden), F32)] + [shape((2, share, hidden), BF16)] * peers,
        [SMEM, VMEM, VMEM],
        [pltpu.VMEM((domains, share, hidden), F32)],
        nbytes=narrow * hidden * 8,
        name="weight_shares",
    )(ids, keep, recv)
    terms, _ = lax.optimization_barrier((terms, shares))
    shares = exchange([None] + shares, "dom")[1:]
    crossing = call(
        functools.partial(sum_mirror, slots, at),
        shape((offers * tile + EXTRA, wide), BF16),
        [SMEM] + [VMEM] * (2 + peers),
        [pltpu.VMEM((offers, tile, wide), F32)],
        nbytes=4 * domains * slots * tile * wide,
        name="sum_mirror",
    )(tab, bias_here, kept, *terms)
    returned = swap(crossing, "dom", half)
    shares, _ = lax.optimization_barrier((shares, crossing))
    here = call(
        sum_half,
        shape((2, share, hidden), BF16),
        [VMEM] * half,
        nbytes=2 * half * share * hidden * 2,
        name="sum_half",
    )(kept_shares, *shares)
    there = swap(here, "dom", half)
    own, _ = lax.optimization_barrier((own, here))
    back = call(
        functools.partial(back_local, per_row, at),
        shape((blocks, tile, wide), F32),
        [SMEM, VMEM, VMEM],
        flops=2 * blocks * per_row * tile * tile * wide,
        nbytes=blocks * tile * wide * 6,
        name="back_local",
    )(tab, bank_t, own)
    there, back = lax.optimization_barrier((there, back))
    summed = call(
        functools.partial(sum_both, norm_scale),
        shape((2, share, hidden), BF16),
        [VMEM, VMEM],
        nbytes=6 * share * hidden * 2,
        name="sum_both",
    )(here, there)
    gathered = exchange([summed] * half, "dom")
    hid = call(
        functools.partial(finish_nodes, half, slots, norm_scale, at),
        [shape((rows_here + EXTRA, wide), BF16)] * groups,
        [SMEM, VMEM, VMEM, VMEM] + [VMEM] * peers,
        [pltpu.VMEM((blocks, tile, wide), F32)],
        nbytes=domains * slots * tile * wide * 2 + blocks * tile * wide * 6,
        name="finish_nodes",
    )(tab, back, bias_here, returned, *terms)
    hid = exchange(hid, "grp")
    gathered, hid = lax.optimization_barrier((gathered, hid))
    grad_nodes, grad_bias = call(
        functools.partial(node_grads, groups),
        [shape((rows_here, embed), BF16), shape((1, hidden), F32)],
        [SMEM, VMEM] + [VMEM] * groups,
        [pltpu.VMEM((groups, rows_here + EXTRA, wide), BF16)],
        flops=2 * rows_here * embed * hidden,
        nbytes=embed * hidden * 2 + rows_here * (embed + hidden) * 2,
        name="node_grads",
    )(ids, weight, *hid)
    joined = call(
        join_shares,
        shape((domains, share, hidden), BF16),
        [SMEM] + [VMEM] * half,
        nbytes=4 * narrow * hidden,
        name="join_shares",
    )(ids, *gathered).reshape(narrow, hidden)
    count = groups // 2

    def place(parts, masks, before=()):
        return call(
            functools.partial(place_weight, masks),
            out_shape=shape((embed, hidden), F32),
            specs=[SMEM] + [VMEM] * len(parts) + [pl.BlockSpec(memory_space=pl.ANY)] * len(before),
            scratch=[
                pltpu.VMEM((len(parts), narrow, hidden), F32),
                pltpu.SemaphoreType.DMA((len(parts), COPIES)),
            ],
            nbytes=embed * hidden * 3,
            name="place_weight",
            out_specs=pl.BlockSpec(memory_space=pl.ANY),
            aliases={len(parts) + 1: 0} if before else {},
        )(ids, *parts, *before)

    across = swap(joined, "grp", count)
    parts, masks = spread(joined, "grp", count // 2)
    grad_weight = place(parts, masks)
    across, grad_weight, grad_nodes = lax.optimization_barrier((across, grad_weight, grad_nodes))
    parts, masks = spread(across, "grp", count // 2)
    grad_weight = place([across], [count], [grad_weight])
    grad_weight = place(parts[1:], [mask + count for mask in masks[1:]], [grad_weight])
    return (activations, grad_nodes, grad_weight, grad_bias.reshape(hidden))


def solution(mesh):
    in_specs = (
        P(("dom", "grp"), None),
        P(),
        P(),
        P(("dom", "grp"), None),
        P(),
        P("dom", None, None),
        P("dom", None, None),
        P("dom", None),
        P(),
        P("dom", None, None),
        P("dom", None, None),
    )
    out_specs = (P(("dom", "grp"), None), P(("dom", "grp"), None), P(), P())
    return jax.shard_map(
        per_device, mesh=mesh, in_specs=in_specs, out_specs=out_specs, check_vma=False
    )
```

profile of v0, /device:TPU:0, one launch (start us, length us, event | category | flops | bytes accessed | tf_op | source)
XLA Modules:
  0.0 102.2 jit_solution(2619577333115599218)
XLA Ops:
  2.4 2.5 %collective-permute-start = (bf16[256,256]{1,0:T(8,128)(2,1)S(1)}, bf16[256,256]{1,0:T(8,128)(2,1)S(1)}, u32[]{:S(2)}, u32[]{:S(2)}) collective-permute-start(bf16[256,256]{1,0:T(8,128)(2,1)S(1)} %get-tuple-element.81), channel_id=1, source_target_pairs={{0,3},{1,2},{2,1},{3,0},{4,7},{5,6},{6,5},{7,4},{8,11},{9,10},{10,... | collective-permute-start | bytes 393224 | tf_op jit(solution)/shard_map/ppermute | solution.py:53
  12.4 3.4 %collective-permute-start.3 = (bf16[4,128,256]{2,1,0:T(8,128)(2,1)S(1)}, bf16[4,128,256]{2,1,0:T(8,128)(2,1)S(1)}, u32[]{:S(2)}, u32[]{:S(2)}) collective-permute-start(bf16[4,128,256]{2,1,0:T(8,128)(2,1)S(1)} %get-tuple-element.85), channel_id=1, source_target_pairs={{0,16},{4,20},{8,24},{12,28},{16,0},{20,4},{24,8},{28,12},{1,17},{... | collective-permute-start | bytes 786440 | tf_op jit(solution)/shard_map/ppermute | solution.py:53
  15.9 1.5 %collective-permute-start.7 = (bf16[256,256]{1,0:T(8,128)(2,1)S(1)}, bf16[256,256]{1,0:T(8,128)(2,1)S(1)}, u32[]{:S(2)}, u32[]{:S(2)}) collective-permute-start(bf16[256,256]{1,0:T(8,128)(2,1)S(1)} %get-tuple-element.92), channel_id=1, source_target_pairs={{0,4},{4,0},{8,12},{12,8},{16,20},{20,16},{24,28},{28,24},{1,5},{5... | collective-permute-start | bytes 393224 | tf_op jit(solution)/shard_map/ppermute | solution.py:53
  17.3 1.6 %collective-permute-start.8 = (bf16[256,256]{1,0:T(8,128)(2,1)S(1)}, bf16[256,256]{1,0:T(8,128)(2,1)S(1)}, u32[]{:S(2)}, u32[]{:S(2)}) collective-permute-start(bf16[256,256]{1,0:T(8,128)(2,1)S(1)} %get-tuple-element.93), channel_id=1, source_target_pairs={{0,8},{4,12},{8,0},{12,4},{16,24},{20,28},{24,16},{28,20},{1,9},{5... | collective-permute-start | bytes 393224 | tf_op jit(solution)/shard_map/ppermute | solution.py:53
  20.4 3.1 %local_sum.1.local = f32[8,128,256]{2,1,0:T(8,128)S(1)} custom-call(s32[342]{0:T(512)S(1)} %concatenate.4.tab, bf16[16,128,128]{2,1,0:T(8,128)(2,1)S(1)} %copy-done, bf16[8,128,256]{2,1,0:T(8,128)(2,1)S(1)} %get-tuple-element.86.x), custom_call_target="tpu_custom_call" | custom-call | flops 1073741824 | bytes 1572864 | tf_op jit(solution)/shard_map/local_sum/pallas_call | solution.py:436
  23.5 4.6 %collective-permute-done.3.offered.mirrored = bf16[4,128,256]{2,1,0:T(8,128)(2,1)S(1)} collective-permute-done((bf16[4,128,256]{2,1,0:T(8,128)(2,1)S(1)}, bf16[4,128,256]{2,1,0:T(8,128)(2,1)S(1)}, u32[]{:S(2)}, u32[]{:S(2)}) %collective-permute-start.3) | collective-permute-done | bytes 262176 | tf_op jit(solution)/shard_map/ppermute | solution.py:53
  28.7 1.6 %collective-permute-start.4 = (bf16[256,256]{1,0:T(8,128)(2,1)S(1)}, bf16[256,256]{1,0:T(8,128)(2,1)S(1)}, u32[]{:S(2)}, u32[]{:S(2)}) collective-permute-start(bf16[256,256]{1,0:T(8,128)(2,1)S(1)} %get-tuple-element.88), channel_id=1, source_target_pairs={{0,4},{4,0},{8,12},{12,8},{16,20},{20,16},{24,28},{28,24},{1,5},{5... | collective-permute-start | bytes 393224 | tf_op jit(solution)/shard_map/ppermute | solution.py:53
  30.9 1.4 %collective-permute-start.6 = (bf16[256,256]{1,0:T(8,128)(2,1)S(1)}, bf16[256,256]{1,0:T(8,128)(2,1)S(1)}, u32[]{:S(2)}, u32[]{:S(2)}) collective-permute-start(bf16[256,256]{1,0:T(8,128)(2,1)S(1)} %get-tuple-element.90), channel_id=1, source_target_pairs={{0,12},{4,8},{8,4},{12,0},{16,28},{20,24},{24,20},{28,16},{1,13},{... | collective-permute-start | bytes 393224 | tf_op jit(solution)/shard_map/ppermute | solution.py:53
  32.3 1.4 %add_near.1.local = f32[8,128,256]{2,1,0:T(8,128)S(1)} custom-call(s32[342]{0:T(512)S(1)} %concatenate.4.tab, bf16[16,128,128]{2,1,0:T(8,128)(2,1)S(1)} %copy-done.1, f32[8,128,256]{2,1,0:T(8,128)S(1)} %local_sum.1.local, bf16[4,128,256]{2,1,0:T(8,128)(2,1)S(1)} %collective-permute-done.3.offered.mirrored, ...), custom_call_target="tpu_custom_call" | custom-call | flops 67108864 | bytes 2097152 | tf_op jit(solution)/shard_map/add_near/pallas_call | solution.py:453
  34.1 1.9 %collective-permute-done.5.refs_1_ = bf16[256,256]{1,0:T(8,128)(2,1)S(1)} collective-permute-done((bf16[256,256]{1,0:T(8,128)(2,1)S(1)}, bf16[256,256]{1,0:T(8,128)(2,1)S(1)}, u32[]{:S(2)}, u32[]{:S(2)}) %collective-permute-start.5) | collective-permute-done | bytes 131104 | tf_op jit(solution)/shard_map/ppermute | solution.py:53
  36.0 2.0 %collective-permute-done.6.refs_2_ = bf16[256,256]{1,0:T(8,128)(2,1)S(1)} collective-permute-done((bf16[256,256]{1,0:T(8,128)(2,1)S(1)}, bf16[256,256]{1,0:T(8,128)(2,1)S(1)}, u32[]{:S(2)}, u32[]{:S(2)}) %collective-permute-start.6) | collective-permute-done | bytes 131104 | tf_op jit(solution)/shard_map/ppermute | solution.py:53
  39.4 1.7 %collective-permute-start.11 = (bf16[256,256]{1,0:T(8,128)(2,1)S(1)}, bf16[256,256]{1,0:T(8,128)(2,1)S(1)}, u32[]{:S(2)}, u32[]{:S(2)}) collective-permute-start(bf16[256,256]{1,0:T(8,128)(2,1)S(1)} %get-tuple-element.101), channel_id=1, source_target_pairs={{0,2},{1,3},{2,0},{3,1},{4,6},{5,7},{6,4},{7,5},{8,10},{9,11},{10,... | collective-permute-start | bytes 393224 | tf_op jit(solution)/shard_map/ppermute | solution.py:53
  41.2 4.5 %collective-permute-done.11.refs_2_ = bf16[256,256]{1,0:T(8,128)(2,1)S(1)} collective-permute-done((bf16[256,256]{1,0:T(8,128)(2,1)S(1)}, bf16[256,256]{1,0:T(8,128)(2,1)S(1)}, u32[]{:S(2)}, u32[]{:S(2)}) %collective-permute-start.11) | collective-permute-done | bytes 131104 | tf_op jit(solution)/shard_map/ppermute | solution.py:53
  45.7 1.9 %collective-permute-done.12.refs_3_ = bf16[256,256]{1,0:T(8,128)(2,1)S(1)} collective-permute-done((bf16[256,256]{1,0:T(8,128)(2,1)S(1)}, bf16[256,256]{1,0:T(8,128)(2,1)S(1)}, u32[]{:S(2)}, u32[]{:S(2)}) %collective-permute-start.12) | collective-permute-done | bytes 131104 | tf_op jit(solution)/shard_map/ppermute | solution.py:53
  49.7 1.6 %collective-permute-start.15 = (bf16[256,128]{1,0:T(8,128)(2,1)S(1)}, bf16[256,128]{1,0:T(8,128)(2,1)S(1)}, u32[]{:S(2)}, u32[]{:S(2)}) collective-permute-start(bf16[256,128]{1,0:T(8,128)(2,1)S(1)} %get-tuple-element.107), channel_id=1, source_target_pairs={{0,2},{1,3},{2,0},{3,1},{4,6},{5,7},{6,4},{7,5},{8,10},{9,11},{10,... | collective-permute-start | bytes 196616 | tf_op jit(solution)/shard_map/ppermute | solution.py:53
  52.1 1.9 %collective-permute-done.15.refs_2_ = bf16[256,128]{1,0:T(8,128)(2,1)S(1)} collective-permute-done((bf16[256,128]{1,0:T(8,128)(2,1)S(1)}, bf16[256,128]{1,0:T(8,128)(2,1)S(1)}, u32[]{:S(2)}, u32[]{:S(2)}) %collective-permute-start.15) | collective-permute-done | bytes 65568 | tf_op jit(solution)/shard_map/ppermute | solution.py:53
  54.0 1.6 %collective-permute-done.16.refs_3_ = bf16[256,128]{1,0:T(8,128)(2,1)S(1)} collective-permute-done((bf16[256,128]{1,0:T(8,128)(2,1)S(1)}, bf16[256,128]{1,0:T(8,128)(2,1)S(1)}, u32[]{:S(2)}, u32[]{:S(2)}) %collective-permute-start.16) | collective-permute-done | bytes 65568 | tf_op jit(solution)/shard_map/ppermute | solution.py:53
  58.4 1.7 %collective-permute-start.22 = (bf16[528,128]{1,0:T(8,128)(2,1)S(1)}, bf16[528,128]{1,0:T(8,128)(2,1)S(1)}, u32[]{:S(2)}, u32[]{:S(2)}) collective-permute-start(bf16[528,128]{1,0:T(8,128)(2,1)S(1)} %get-tuple-element.129), channel_id=1, source_target_pairs={{0,8},{4,12},{8,0},{12,4},{16,24},{20,28},{24,16},{28,20},{1,9},{5... | collective-permute-start | bytes 405512 | tf_op jit(solution)/shard_map/ppermute | solution.py:53
  61.3 2.2 %collective-permute-done.18.refs_0_ = bf16[528,128]{1,0:T(8,128)(2,1)S(1)} collective-permute-done((bf16[528,128]{1,0:T(8,128)(2,1)S(1)}, bf16[528,128]{1,0:T(8,128)(2,1)S(1)}, u32[]{:S(2)}, u32[]{:S(2)}) %collective-permute-start.18) | collective-permute-done | bytes 135200 | tf_op jit(solution)/shard_map/ppermute | solution.py:53
  65.4 1.6 %collective-permute-start.20 = (bf16[2,32,512]{2,1,0:T(8,128)(2,1)S(1)}, bf16[2,32,512]{2,1,0:T(8,128)(2,1)S(1)}, u32[]{:S(2)}, u32[]{:S(2)}) collective-permute-start(bf16[2,32,512]{2,1,0:T(8,128)(2,1)S(1)} %get-tuple-element.124), channel_id=1, source_target_pairs={{0,8},{4,12},{8,0},{12,4},{16,24},{20,28},{24,16},{28,20},{1,9},{5... | collective-permute-start | bytes 196616 | tf_op jit(solution)/shard_map/ppermute | solution.py:53
  68.9 2.7 %collective-permute-start.28 = (bf16[528,128]{1,0:T(8,128)(2,1)S(1)}, bf16[528,128]{1,0:T(8,128)(2,1)S(1)}, u32[]{:S(2)}, u32[]{:S(2)}) collective-permute-start(bf16[528,128]{1,0:T(8,128)(2,1)S(1)} %sum_mirror.1), channel_id=1, source_target_pairs={{0,16},{4,20},{8,24},{12,28},{16,0},{20,4},{24,8},{28,12},{1,17},{... | collective-permute-start | bytes 405512 | tf_op jit(solution)/shard_map/ppermute | solution.py:53
  71.6 2.0 %collective-permute-done.21.refs_2_ = bf16[2,32,512]{2,1,0:T(8,128)(2,1)S(1)} collective-permute-done((bf16[2,32,512]{2,1,0:T(8,128)(2,1)S(1)}, bf16[2,32,512]{2,1,0:T(8,128)(2,1)S(1)}, u32[]{:S(2)}, u32[]{:S(2)}) %collective-permute-start.21) | collective-permute-done | bytes 65568 | tf_op jit(solution)/shard_map/ppermute | solution.py:53
  73.7 2.4 %collective-permute-start.24 = (bf16[2,32,512]{2,1,0:T(8,128)(2,1)S(1)}, bf16[2,32,512]{2,1,0:T(8,128)(2,1)S(1)}, u32[]{:S(2)}, u32[]{:S(2)}) collective-permute-start(bf16[2,32,512]{2,1,0:T(8,128)(2,1)S(1)} %sum_half.1.here), channel_id=1, source_target_pairs={{0,16},{4,20},{8,24},{12,28},{16,0},{20,4},{24,8},{28,12},{1,17},{... | collective-permute-start | bytes 196616 | tf_op jit(solution)/shard_map/ppermute | solution.py:53
  76.1 3.0 %back_local.1.local = f32[8,128,128]{2,1,0:T(8,128)S(1)} custom-call(s32[342]{0:T(512)S(1)} %concatenate.4.tab, bf16[16,128,128]{2,1,0:T(8,128)(2,1)S(1)} %bitcast.8, bf16[8,128,128]{2,1,0:T(8,128)(2,1)S(1)} %get-tuple-element.138.own), custom_call_target="tpu_custom_call" | custom-call | flops 536870912 | bytes 786432 | tf_op jit(solution)/shard_map/back_local/pallas_call | solution.py:561
  81.8 1.6 %collective-permute-start.30 = (bf16[272,128]{1,0:T(8,128)(2,1)S(1)}, bf16[272,128]{1,0:T(8,128)(2,1)S(1)}, u32[]{:S(2)}, u32[]{:S(2)}) collective-permute-start(bf16[272,128]{1,0:T(8,128)(2,1)S(1)} %get-tuple-element.143), channel_id=1, source_target_pairs={{0,2},{1,3},{2,0},{3,1},{4,6},{5,7},{6,4},{7,5},{8,10},{9,11},{10,... | collective-permute-start | bytes 208904 | tf_op jit(solution)/shard_map/ppermute | solution.py:53
  84.4 1.8 %collective-permute-start.27 = (bf16[2,32,512]{2,1,0:T(8,128)(2,1)S(1)}, bf16[2,32,512]{2,1,0:T(8,128)(2,1)S(1)}, u32[]{:S(2)}, u32[]{:S(2)}) collective-permute-start(bf16[2,32,512]{2,1,0:T(8,128)(2,1)S(1)} %sum_both.1.refs_0_), channel_id=1, source_target_pairs={{0,12},{4,8},{8,4},{12,0},{16,28},{20,24},{24,20},{28,16},{1,13},{... | collective-permute-start | bytes 196616 | tf_op jit(solution)/shard_map/ppermute | solution.py:53
  86.2 2.4 %collective-permute-done.26.refs_2_ = bf16[2,32,512]{2,1,0:T(8,128)(2,1)S(1)} collective-permute-done((bf16[2,32,512]{2,1,0:T(8,128)(2,1)S(1)}, bf16[2,32,512]{2,1,0:T(8,128)(2,1)S(1)}, u32[]{:S(2)}, u32[]{:S(2)}) %collective-permute-start.26) | collective-permute-done | bytes 65568 | tf_op jit(solution)/shard_map/ppermute | solution.py:53
  90.5 1.4 %collective-permute-start.32 = (bf16[256,512]{1,0:T(8,128)(2,1)S(1)}, bf16[256,512]{1,0:T(8,128)(2,1)S(1)}, u32[]{:S(2)}, u32[]{:S(2)}) collective-permute-start(bf16[256,512]{1,0:T(8,128)(2,1)S(1)} %bitcast.10), channel_id=1, source_target_pairs={{0,2},{1,3},{2,0},{3,1},{4,6},{5,7},{6,4},{7,5},{8,10},{9,11},{10,... | collective-permute-start | bytes 786440 | tf_op jit(solution)/shard_map/ppermute | solution.py:53
  92.0 1.8 %node_grads.1 = (bf16[256,1024]{1,0:T(8,128)(2,1)}, f32[1,512]{1,0:T(1,128)}) custom-call(s32[2]{0:T(128)S(1)} %pad_add_fusion.ids, bf16[1024,512]{1,0:T(8,128)(2,1)S(1)} %copy-done.2, bf16[272,128]{1,0:T(8,128)(2,1)S(1)} %get-tuple-element.149.refs_0_, bf16[272,128]{1,0:T(8,128)(2,1)S(1)} %collective-permute-done.29.refs_1_, ...), custom_call_target="tpu_custom_call" | custom-call | flops 268435456 | bytes 1835008 | tf_op jit(solution)/shard_map/node_grads/pallas_call | solution.py:588
  93.8 1.6 %place_weight.3.refs_1_ = f32[1024,512]{1,0:T(8,128)} custom-call(s32[2]{0:T(128)S(1)} %pad_add_fusion.ids, bf16[256,512]{1,0:T(8,128)(2,1)S(1)} %bitcast.11, bf16[256,512]{1,0:T(8,128)(2,1)S(1)} %collective-permute-done.33.refs_1_), custom_call_target="tpu_custom_call" | custom-call | bytes 1572864 | tf_op jit(solution)/shard_map/place_weight/pallas_call | solution.py:607
  95.4 3.9 %collective-permute-done.32.refs_0_ = bf16[256,512]{1,0:T(8,128)(2,1)S(1)} collective-permute-done((bf16[256,512]{1,0:T(8,128)(2,1)S(1)}, bf16[256,512]{1,0:T(8,128)(2,1)S(1)}, u32[]{:S(2)}, u32[]{:S(2)}) %collective-permute-start.32) | collective-permute-done | bytes 262176 | tf_op jit(solution)/shard_map/ppermute | solution.py:53
  99.3 1.4 %place_weight.4.refs_1_ = f32[1024,512]{1,0:T(8,128)} custom-call(s32[2]{0:T(128)S(1)} %pad_add_fusion.ids, bf16[256,512]{1,0:T(8,128)(2,1)S(1)} %collective-permute-done.32.refs_0_, f32[1024,512]{1,0:T(8,128)} %place_weight.3.refs_1_), custom_call_target="tpu_custom_call", output_to_operand_aliasing={{}: (2, {})} | custom-call | bytes 1572864 | tf_op jit(solution)/shard_map/place_weight/pallas_call | solution.py:607
  (88 shorter events, 31.6 us)
Async XLA Ops:
  2.4 9.2 %collective-permute-start = (bf16[256,256]{1,0:T(8,128)(2,1)S(1)}, bf16[256,256]{1,0:T(8,128)(2,1)S(1)}, u32[]{:S(2)}, u32[]{:S(2)}) collective-permute-start(bf16[256,256]{1,0:T(8,128)(2,1)S(1)} %get-tuple-element.81), channel_id=1, source_target_pairs={{0,3},{1,2},{2,1},{3,0},{4,7},{5,6},{6,5},{7,4},{8,11},{9,10},{10,... | collective-permute-start | bytes 393224 | tf_op jit(solution)/shard_map/ppermute | solution.py:53
  4.9 6.9 %collective-permute-start.1 = (bf16[256,256]{1,0:T(8,128)(2,1)S(1)}, bf16[256,256]{1,0:T(8,128)(2,1)S(1)}, u32[]{:S(2)}, u32[]{:S(2)}) collective-permute-start(bf16[256,256]{1,0:T(8,128)(2,1)S(1)} %get-tuple-element.82), channel_id=1, source_target_pairs={{0,2},{1,3},{2,0},{3,1},{4,6},{5,7},{6,4},{7,5},{8,10},{9,11},{10,... | collective-permute-start | bytes 393224 | tf_op jit(solution)/shard_map/ppermute | solution.py:53
  5.5 6.2 %collective-permute-start.2 = (bf16[256,256]{1,0:T(8,128)(2,1)S(1)}, bf16[256,256]{1,0:T(8,128)(2,1)S(1)}, u32[]{:S(2)}, u32[]{:S(2)}) collective-permute-start(bf16[256,256]{1,0:T(8,128)(2,1)S(1)} %get-tuple-element.83), channel_id=1, source_target_pairs={{0,1},{1,0},{2,3},{3,2},{4,5},{5,4},{6,7},{7,6},{8,9},{9,8},{10,11... | collective-permute-start | bytes 393224 | tf_op jit(solution)/shard_map/ppermute | solution.py:53
  12.4 15.7 %collective-permute-start.3 = (bf16[4,128,256]{2,1,0:T(8,128)(2,1)S(1)}, bf16[4,128,256]{2,1,0:T(8,128)(2,1)S(1)}, u32[]{:S(2)}, u32[]{:S(2)}) collective-permute-start(bf16[4,128,256]{2,1,0:T(8,128)(2,1)S(1)} %get-tuple-element.85), channel_id=1, source_target_pairs={{0,16},{4,20},{8,24},{12,28},{16,0},{20,4},{24,8},{28,12},{1,17},{... | collective-permute-start | bytes 786440 | tf_op jit(solution)/shard_map/ppermute | solution.py:53
  15.9 15.0 %collective-permute-start.7 = (bf16[256,256]{1,0:T(8,128)(2,1)S(1)}, bf16[256,256]{1,0:T(8,128)(2,1)S(1)}, u32[]{:S(2)}, u32[]{:S(2)}) collective-permute-start(bf16[256,256]{1,0:T(8,128)(2,1)S(1)} %get-tuple-element.92), channel_id=1, source_target_pairs={{0,4},{4,0},{8,12},{12,8},{16,20},{20,16},{24,28},{28,24},{1,5},{5... | collective-permute-start | bytes 393224 | tf_op jit(solution)/shard_map/ppermute | solution.py:53
  17.3 15.0 %collective-permute-start.8 = (bf16[256,256]{1,0:T(8,128)(2,1)S(1)}, bf16[256,256]{1,0:T(8,128)(2,1)S(1)}, u32[]{:S(2)}, u32[]{:S(2)}) collective-permute-start(bf16[256,256]{1,0:T(8,128)(2,1)S(1)} %get-tuple-element.93), channel_id=1, source_target_pairs={{0,8},{4,12},{8,0},{12,4},{16,24},{20,28},{24,16},{28,20},{1,9},{5... | collective-permute-start | bytes 393224 | tf_op jit(solution)/shard_map/ppermute | solution.py:53
  18.9 13.4 %collective-permute-start.9 = (bf16[256,256]{1,0:T(8,128)(2,1)S(1)}, bf16[256,256]{1,0:T(8,128)(2,1)S(1)}, u32[]{:S(2)}, u32[]{:S(2)}) collective-permute-start(bf16[256,256]{1,0:T(8,128)(2,1)S(1)} %get-tuple-element.94), channel_id=1, source_target_pairs={{0,12},{4,8},{8,4},{12,0},{16,28},{20,24},{24,20},{28,16},{1,13},{... | collective-permute-start | bytes 393224 | tf_op jit(solution)/shard_map/ppermute | solution.py:53
  28.7 5.4 %collective-permute-start.4 = (bf16[256,256]{1,0:T(8,128)(2,1)S(1)}, bf16[256,256]{1,0:T(8,128)(2,1)S(1)}, u32[]{:S(2)}, u32[]{:S(2)}) collective-permute-start(bf16[256,256]{1,0:T(8,128)(2,1)S(1)} %get-tuple-element.88), channel_id=1, source_target_pairs={{0,4},{4,0},{8,12},{12,8},{16,20},{20,16},{24,28},{28,24},{1,5},{5... | collective-permute-start | bytes 393224 | tf_op jit(solution)/shard_map/ppermute | solution.py:53
  30.3 5.7 %collective-permute-start.5 = (bf16[256,256]{1,0:T(8,128)(2,1)S(1)}, bf16[256,256]{1,0:T(8,128)(2,1)S(1)}, u32[]{:S(2)}, u32[]{:S(2)}) collective-permute-start(bf16[256,256]{1,0:T(8,128)(2,1)S(1)} %get-tuple-element.89), channel_id=1, source_target_pairs={{0,8},{4,12},{8,0},{12,4},{16,24},{20,28},{24,16},{28,20},{1,9},{5... | collective-permute-start | bytes 393224 | tf_op jit(solution)/shard_map/ppermute | solution.py:53
  30.9 7.1 %collective-permute-start.6 = (bf16[256,256]{1,0:T(8,128)(2,1)S(1)}, bf16[256,256]{1,0:T(8,128)(2,1)S(1)}, u32[]{:S(2)}, u32[]{:S(2)}) collective-permute-start(bf16[256,256]{1,0:T(8,128)(2,1)S(1)} %get-tuple-element.90), channel_id=1, source_target_pairs={{0,12},{4,8},{8,4},{12,0},{16,28},{20,24},{24,20},{28,16},{1,13},{... | collective-permute-start | bytes 393224 | tf_op jit(solution)/shard_map/ppermute | solution.py:53
  39.4 6.4 %collective-permute-start.11 = (bf16[256,256]{1,0:T(8,128)(2,1)S(1)}, bf16[256,256]{1,0:T(8,128)(2,1)S(1)}, u32[]{:S(2)}, u32[]{:S(2)}) collective-permute-start(bf16[256,256]{1,0:T(8,128)(2,1)S(1)} %get-tuple-element.101), channel_id=1, source_target_pairs={{0,2},{1,3},{2,0},{3,1},{4,6},{5,7},{6,4},{7,5},{8,10},{9,11},{10,... | collective-permute-start | bytes 393224 | tf_op jit(solution)/shard_map/ppermute | solution.py:53
  41.1 6.6 %collective-permute-start.12 = (bf16[256,256]{1,0:T(8,128)(2,1)S(1)}, bf16[256,256]{1,0:T(8,128)(2,1)S(1)}, u32[]{:S(2)}, u32[]{:S(2)}) collective-permute-start(bf16[256,256]{1,0:T(8,128)(2,1)S(1)} %get-tuple-element.102), channel_id=1, source_target_pairs={{0,3},{1,2},{2,1},{3,0},{4,7},{5,6},{6,5},{7,4},{8,11},{9,10},{10,... | collective-permute-start | bytes 393224 | tf_op jit(solution)/shard_map/ppermute | solution.py:53
  49.2 6.4 %collective-permute-start.13 = (bf16[2,256,512]{2,1,0:T(8,128)(2,1)S(1)}, bf16[2,256,512]{2,1,0:T(8,128)(2,1)S(1)}, u32[]{:S(2)}, u32[]{:S(2)}) collective-permute-start(bf16[2,256,512]{2,1,0:T(8,128)(2,1)S(1)} %get-tuple-element.104), channel_id=1, source_target_pairs={{0,1},{1,0},{2,3},{3,2},{4,5},{5,4},{6,7},{7,6},{8,9},{9,8},{10,11... | collective-permute-start | bytes 1572872 | tf_op jit(solution)/shard_map/ppermute | solution.py:53
  49.7 4.3 %collective-permute-start.15 = (bf16[256,128]{1,0:T(8,128)(2,1)S(1)}, bf16[256,128]{1,0:T(8,128)(2,1)S(1)}, u32[]{:S(2)}, u32[]{:S(2)}) collective-permute-start(bf16[256,128]{1,0:T(8,128)(2,1)S(1)} %get-tuple-element.107), channel_id=1, source_target_pairs={{0,2},{1,3},{2,0},{3,1},{4,6},{5,7},{6,4},{7,5},{8,10},{9,11},{10,... | collective-permute-start | bytes 196616 | tf_op jit(solution)/shard_map/ppermute | solution.py:53
  51.4 4.2 %collective-permute-start.16 = (bf16[256,128]{1,0:T(8,128)(2,1)S(1)}, bf16[256,128]{1,0:T(8,128)(2,1)S(1)}, u32[]{:S(2)}, u32[]{:S(2)}) collective-permute-start(bf16[256,128]{1,0:T(8,128)(2,1)S(1)} %get-tuple-element.108), channel_id=1, source_target_pairs={{0,3},{1,2},{2,1},{3,0},{4,7},{5,6},{6,5},{7,4},{8,11},{9,10},{10,... | collective-permute-start | bytes 196616 | tf_op jit(solution)/shard_map/ppermute | solution.py:53
  55.7 8.4 %collective-permute-start.17 = (bf16[1,256,512]{2,1,0:T(8,128)(2,1)S(1)}, bf16[1,256,512]{2,1,0:T(8,128)(2,1)S(1)}, u32[]{:S(2)}, u32[]{:S(2)}) collective-permute-start(bf16[1,256,512]{2,1,0:T(8,128)(2,1)S(1)} %get-tuple-element.114), channel_id=1, source_target_pairs={{0,2},{1,3},{2,0},{3,1},{4,6},{5,7},{6,4},{7,5},{8,10},{9,11},{10,... | collective-permute-start | bytes 786440 | tf_op jit(solution)/shard_map/ppermute | solution.py:53
  57.8 5.7 %collective-permute-start.18 = (bf16[528,128]{1,0:T(8,128)(2,1)S(1)}, bf16[528,128]{1,0:T(8,128)(2,1)S(1)}, u32[]{:S(2)}, u32[]{:S(2)}) collective-permute-start(bf16[528,128]{1,0:T(8,128)(2,1)S(1)} %get-tuple-element.120), channel_id=1, source_target_pairs={{0,4},{4,0},{8,12},{12,8},{16,20},{20,16},{24,28},{28,24},{1,5},{5... | collective-permute-start | bytes 405512 | tf_op jit(solution)/shard_map/ppermute | solution.py:53
  58.4 9.9 %collective-permute-start.22 = (bf16[528,128]{1,0:T(8,128)(2,1)S(1)}, bf16[528,128]{1,0:T(8,128)(2,1)S(1)}, u32[]{:S(2)}, u32[]{:S(2)}) collective-permute-start(bf16[528,128]{1,0:T(8,128)(2,1)S(1)} %get-tuple-element.129), channel_id=1, source_target_pairs={{0,8},{4,12},{8,0},{12,4},{16,24},{20,28},{24,16},{28,20},{1,9},{5... | collective-permute-start | bytes 405512 | tf_op jit(solution)/shard_map/ppermute | solution.py:53
  60.1 8.2 %collective-permute-start.23 = (bf16[528,128]{1,0:T(8,128)(2,1)S(1)}, bf16[528,128]{1,0:T(8,128)(2,1)S(1)}, u32[]{:S(2)}, u32[]{:S(2)}) collective-permute-start(bf16[528,128]{1,0:T(8,128)(2,1)S(1)} %get-tuple-element.130), channel_id=1, source_target_pairs={{0,12},{4,8},{8,4},{12,0},{16,28},{20,24},{24,20},{28,16},{1,13},{... | collective-permute-start | bytes 405512 | tf_op jit(solution)/shard_map/ppermute | solution.py:53
  64.7 6.9 %collective-permute-start.19 = (bf16[2,32,512]{2,1,0:T(8,128)(2,1)S(1)}, bf16[2,32,512]{2,1,0:T(8,128)(2,1)S(1)}, u32[]{:S(2)}, u32[]{:S(2)}) collective-permute-start(bf16[2,32,512]{2,1,0:T(8,128)(2,1)S(1)} %get-tuple-element.123), channel_id=1, source_target_pairs={{0,4},{4,0},{8,12},{12,8},{16,20},{20,16},{24,28},{28,24},{1,5},{5... | collective-permute-start | bytes 196616 | tf_op jit(solution)/shard_map/ppermute | solution.py:53
  65.4 6.2 %collective-permute-start.20 = (bf16[2,32,512]{2,1,0:T(8,128)(2,1)S(1)}, bf16[2,32,512]{2,1,0:T(8,128)(2,1)S(1)}, u32[]{:S(2)}, u32[]{:S(2)}) collective-permute-start(bf16[2,32,512]{2,1,0:T(8,128)(2,1)S(1)} %get-tuple-element.124), channel_id=1, source_target_pairs={{0,8},{4,12},{8,0},{12,4},{16,24},{20,28},{24,16},{28,20},{1,9},{5... | collective-permute-start | bytes 196616 | tf_op jit(solution)/shard_map/ppermute | solution.py:53
  67.0 6.6 %collective-permute-start.21 = (bf16[2,32,512]{2,1,0:T(8,128)(2,1)S(1)}, bf16[2,32,512]{2,1,0:T(8,128)(2,1)S(1)}, u32[]{:S(2)}, u32[]{:S(2)}) collective-permute-start(bf16[2,32,512]{2,1,0:T(8,128)(2,1)S(1)} %get-tuple-element.125), channel_id=1, source_target_pairs={{0,12},{4,8},{8,4},{12,0},{16,28},{20,24},{24,20},{28,16},{1,13},{... | collective-permute-start | bytes 196616 | tf_op jit(solution)/shard_map/ppermute | solution.py:53
  68.9 12.1 %collective-permute-start.28 = (bf16[528,128]{1,0:T(8,128)(2,1)S(1)}, bf16[528,128]{1,0:T(8,128)(2,1)S(1)}, u32[]{:S(2)}, u32[]{:S(2)}) collective-permute-start(bf16[528,128]{1,0:T(8,128)(2,1)S(1)} %sum_mirror.1), channel_id=1, source_target_pairs={{0,16},{4,20},{8,24},{12,28},{16,0},{20,4},{24,8},{28,12},{1,17},{... | collective-permute-start | bytes 405512 | tf_op jit(solution)/shard_map/ppermute | solution.py:53
  73.7 6.2 %collective-permute-start.24 = (bf16[2,32,512]{2,1,0:T(8,128)(2,1)S(1)}, bf16[2,32,512]{2,1,0:T(8,128)(2,1)S(1)}, u32[]{:S(2)}, u32[]{:S(2)}) collective-permute-start(bf16[2,32,512]{2,1,0:T(8,128)(2,1)S(1)} %sum_half.1.here), channel_id=1, source_target_pairs={{0,16},{4,20},{8,24},{12,28},{16,0},{20,4},{24,8},{28,12},{1,17},{... | collective-permute-start | bytes 196616 | tf_op jit(solution)/shard_map/ppermute | solution.py:53
  79.9 4.5 %collective-permute-start.25 = (bf16[2,32,512]{2,1,0:T(8,128)(2,1)S(1)}, bf16[2,32,512]{2,1,0:T(8,128)(2,1)S(1)}, u32[]{:S(2)}, u32[]{:S(2)}) collective-permute-start(bf16[2,32,512]{2,1,0:T(8,128)(2,1)S(1)} %sum_both.1.refs_0_), channel_id=1, source_target_pairs={{0,4},{4,0},{8,12},{12,8},{16,20},{20,16},{24,28},{28,24},{1,5},{5... | collective-permute-start | bytes 196616 | tf_op jit(solution)/shard_map/ppermute | solution.py:53
  81.7 8.1 %collective-permute-start.29 = (bf16[272,128]{1,0:T(8,128)(2,1)S(1)}, bf16[272,128]{1,0:T(8,128)(2,1)S(1)}, u32[]{:S(2)}, u32[]{:S(2)}) collective-permute-start(bf16[272,128]{1,0:T(8,128)(2,1)S(1)} %get-tuple-element.142), channel_id=1, source_target_pairs={{0,1},{1,0},{2,3},{3,2},{4,5},{5,4},{6,7},{7,6},{8,9},{9,8},{10,11... | collective-permute-start | bytes 208904 | tf_op jit(solution)/shard_map/ppermute | solution.py:53
  81.8 8.1 %collective-permute-start.30 = (bf16[272,128]{1,0:T(8,128)(2,1)S(1)}, bf16[272,128]{1,0:T(8,128)(2,1)S(1)}, u32[]{:S(2)}, u32[]{:S(2)}) collective-permute-start(bf16[272,128]{1,0:T(8,128)(2,1)S(1)} %get-tuple-element.143), channel_id=1, source_target_pairs={{0,2},{1,3},{2,0},{3,1},{4,6},{5,7},{6,4},{7,5},{8,10},{9,11},{10,... | collective-permute-start | bytes 208904 | tf_op jit(solution)/shard_map/ppermute | solution.py:53
  83.4 6.5 %collective-permute-start.31 = (bf16[272,128]{1,0:T(8,128)(2,1)S(1)}, bf16[272,128]{1,0:T(8,128)(2,1)S(1)}, u32[]{:S(2)}, u32[]{:S(2)}) collective-permute-start(bf16[272,128]{1,0:T(8,128)(2,1)S(1)} %get-tuple-element.144), channel_id=1, source_target_pairs={{0,3},{1,2},{2,1},{3,0},{4,7},{5,6},{6,5},{7,4},{8,11},{9,10},{10,... | collective-permute-start | bytes 208904 | tf_op jit(solution)/shard_map/ppermute | solution.py:53
  83.7 4.9 %collective-permute-start.26 = (bf16[2,32,512]{2,1,0:T(8,128)(2,1)S(1)}, bf16[2,32,512]{2,1,0:T(8,128)(2,1)S(1)}, u32[]{:S(2)}, u32[]{:S(2)}) collective-permute-start(bf16[2,32,512]{2,1,0:T(8,128)(2,1)S(1)} %sum_both.1.refs_0_), channel_id=1, source_target_pairs={{0,8},{4,12},{8,0},{12,4},{16,24},{20,28},{24,16},{28,20},{1,9},{5... | collective-permute-start | bytes 196616 | tf_op jit(solution)/shard_map/ppermute | solution.py:53
  84.4 5.5 %collective-permute-start.27 = (bf16[2,32,512]{2,1,0:T(8,128)(2,1)S(1)}, bf16[2,32,512]{2,1,0:T(8,128)(2,1)S(1)}, u32[]{:S(2)}, u32[]{:S(2)}) collective-permute-start(bf16[2,32,512]{2,1,0:T(8,128)(2,1)S(1)} %sum_both.1.refs_0_), channel_id=1, source_target_pairs={{0,12},{4,8},{8,4},{12,0},{16,28},{20,24},{24,20},{28,16},{1,13},{... | collective-permute-start | bytes 196616 | tf_op jit(solution)/shard_map/ppermute | solution.py:53
  90.5 3.3 %collective-permute-start.33 = (bf16[256,512]{1,0:T(8,128)(2,1)S(1)}, bf16[256,512]{1,0:T(8,128)(2,1)S(1)}, u32[]{:S(2)}, u32[]{:S(2)}) collective-permute-start(bf16[256,512]{1,0:T(8,128)(2,1)S(1)} %bitcast.9), channel_id=1, source_target_pairs={{0,1},{1,0},{2,3},{3,2},{4,5},{5,4},{6,7},{7,6},{8,9},{9,8},{10,11... | collective-permute-start | bytes 786440 | tf_op jit(solution)/shard_map/ppermute | solution.py:53
  90.5 8.7 %collective-permute-start.32 = (bf16[256,512]{1,0:T(8,128)(2,1)S(1)}, bf16[256,512]{1,0:T(8,128)(2,1)S(1)}, u32[]{:S(2)}, u32[]{:S(2)}) collective-permute-start(bf16[256,512]{1,0:T(8,128)(2,1)S(1)} %bitcast.10), channel_id=1, source_target_pairs={{0,2},{1,3},{2,0},{3,1},{4,6},{5,7},{6,4},{7,5},{8,10},{9,11},{10,... | collective-permute-start | bytes 786440 | tf_op jit(solution)/shard_map/ppermute | solution.py:53
  (9 other events, 70.5 us)
where the time goes:
time: 102 us
  starting transfers between devices  38 us (37%)
  waiting for transfers between devices  32.2 us (32%)
  Pallas kernels  22.6 us (22%)
  local copies, waits for them, and re-layouts  8.41 us (8%)
    ppermute x35, starting transfers between devices, swap(): lax.ppermute(value, axis, [(i, i ^ mask) for i in range(lax.axis_size(axi...  38 us
    ppermute x35, waiting for transfers between devices, swap(): lax.ppermute(value, axis, [(i, i ^ mask) for i in range(lax.axis_size(axi...  32.2 us
    pallas_call x3, Pallas kernels, place(): call(functools.partial(place_weight, masks), out_shape=shape((embed, hidd...  4.31 us
    unnamed x15, local copies, waits for them, and re-layouts  3.89 us
    pallas_call x1, Pallas kernels, per_device(): call(functools.partial(local_sum, per_row, at), shape((blocks, tile, narr...  3.07 us
    pallas_call x1, Pallas kernels, per_device(): call(functools.partial(back_local, per_row, at), shape((blocks, tile, wid...  2.98 us
  transfers between devices with their start and end apart: 35, of which 17 were waited for; matrix products, arithmetic and copies ran while one was open for 6% of the time, Pallas kernels for 16%

commit v1 on v0

--- a/solution.py
+++ b/solution.py
@@ -155,7 +155,7 @@
     per = local.shape[0] // groups
     acc[...] = local[...]
     add = halo_adder(slots, at, tab, bank, acc)
-    for m, block in enumerate(far, half + 1):
+    for m, block in zip(reversed(range(half + 1, 2 * half)), far):
         add(jnp.bitwise_xor(domain, m), lambda s, _, block=block: block[s * tile : (s + 1) * tile])
     for m, out in enumerate(outs):
         owner = jnp.bitwise_xor(group, m)
@@ -467,7 +467,7 @@
         flops=2 * half * slots * tile * tile * narrow,
         nbytes=blocks * tile * narrow * 8,
         name="add_far",
-    )(tab, tile_bank, local, *far)
+    )(tab, tile_bank, local, *reversed(far))
     mine = exchange(aggs, "grp")
     activations, grad, *grads = call(
         functools.partial(dense, groups),
@@ -555,7 +555,7 @@
         [VMEM] * half,
         nbytes=2 * half * share * hidden * 2,
         name="sum_half",
-    )(kept_shares, *shares)
+    )(kept_shares, *reversed(shares))
     there = swap(here, "dom", half)
     own, _ = lax.optimization_barrier((own, here))
     back = call(

time: 102 us -> 102 us (level)
  transfers between devices with their start and end apart: 35 -> 35, of which waited for: 17 -> 16; matrix products, arithmetic and copies ran while one was open for 6% -> 6% of each run, Pallas kernels for 16% -> 16%
where the time goes in v1:
time: 102 us
  starting transfers between devices  37.7 us (37%)
  waiting for transfers between devices  32.1 us (31%)
  Pallas kernels  22.9 us (22%)
  local copies, waits for them, and re-layouts  8.41 us (8%)
    ppermute x35, starting transfers between devices, swap(): lax.ppermute(value, axis, [(i, i ^ mask) for i in range(lax.axis_size(axi...  37.7 us
    ppermute x35, waiting for transfers between devices, swap(): lax.ppermute(value, axis, [(i, i ^ mask) for i in range(lax.axis_size(axi...  32.1 us
    pallas_call x3, Pallas kernels, place(): call(functools.partial(place_weight, masks), out_shape=shape((embed, hidd...  4.31 us
    unnamed x15, local copies, waits for them, and re-layouts  3.89 us
    pallas_call x1, Pallas kernels, per_device(): call(functools.partial(local_sum, per_row, at), shape((blocks, tile, narr...  3.07 us
    pallas_call x1, Pallas kernels, per_device(): call(functools.partial(back_local, per_row, at), shape((blocks, tile, wid...  2.98 us
  transfers between devices with their start and end apart: 35, of which 16 were waited for; matrix products, arithmetic and copies ran while one was open for 6% of the time, Pallas kernels for 16%

profile of v1, /device:TPU:0, one launch (start us, length us, event | category | flops | bytes accessed | tf_op | source)
XLA Modules:
  0.0 102.0 jit_solution(9195458568299860515)
XLA Ops:
  2.4 2.5 %collective-permute-start = (bf16[256,256]{1,0:T(8,128)(2,1)S(1)}, bf16[256,256]{1,0:T(8,128)(2,1)S(1)}, u32[]{:S(2)}, u32[]{:S(2)}) collective-permute-start(bf16[256,256]{1,0:T(8,128)(2,1)S(1)} %get-tuple-element.81), channel_id=1, source_target_pairs={{0,3},{1,2},{2,1},{3,0},{4,7},{5,6},{6,5},{7,4},{8,11},{9,10},{10,... | collective-permute-start | bytes 393224 | tf_op jit(solution)/shard_map/ppermute | solution.py:53
  12.4 3.4 %collective-permute-start.3 = (bf16[4,128,256]{2,1,0:T(8,128)(2,1)S(1)}, bf16[4,128,256]{2,1,0:T(8,128)(2,1)S(1)}, u32[]{:S(2)}, u32[]{:S(2)}) collective-permute-start(bf16[4,128,256]{2,1,0:T(8,128)(2,1)S(1)} %get-tuple-element.85), channel_id=1, source_target_pairs={{0,16},{4,20},{8,24},{12,28},{16,0},{20,4},{24,8},{28,12},{1,17},{... | collective-permute-start | bytes 786440 | tf_op jit(solution)/shard_map/ppermute | solution.py:53
  15.9 1.5 %collective-permute-start.7 = (bf16[256,256]{1,0:T(8,128)(2,1)S(1)}, bf16[256,256]{1,0:T(8,128)(2,1)S(1)}, u32[]{:S(2)}, u32[]{:S(2)}) collective-permute-start(bf16[256,256]{1,0:T(8,128)(2,1)S(1)} %get-tuple-element.92), channel_id=1, source_target_pairs={{0,4},{4,0},{8,12},{12,8},{16,20},{20,16},{24,28},{28,24},{1,5},{5... | collective-permute-start | bytes 393224 | tf_op jit(solution)/shard_map/ppermute | solution.py:53
  17.3 1.6 %collective-permute-start.8 = (bf16[256,256]{1,0:T(8,128)(2,1)S(1)}, bf16[256,256]{1,0:T(8,128)(2,1)S(1)}, u32[]{:S(2)}, u32[]{:S(2)}) collective-permute-start(bf16[256,256]{1,0:T(8,128)(2,1)S(1)} %get-tuple-element.93), channel_id=1, source_target_pairs={{0,8},{4,12},{8,0},{12,4},{16,24},{20,28},{24,16},{28,20},{1,9},{5... | collective-permute-start | bytes 393224 | tf_op jit(solution)/shard_map/ppermute | solution.py:53
  20.4 3.1 %local_sum.1.local = f32[8,128,256]{2,1,0:T(8,128)S(1)} custom-call(s32[342]{0:T(512)S(1)} %concatenate.4.tab, bf16[16,128,128]{2,1,0:T(8,128)(2,1)S(1)} %copy-done, bf16[8,128,256]{2,1,0:T(8,128)(2,1)S(1)} %get-tuple-element.86.x), custom_call_target="tpu_custom_call" | custom-call | flops 1073741824 | bytes 1572864 | tf_op jit(solution)/shard_map/local_sum/pallas_call | solution.py:436
  23.5 4.6 %collective-permute-done.3.offered.mirrored = bf16[4,128,256]{2,1,0:T(8,128)(2,1)S(1)} collective-permute-done((bf16[4,128,256]{2,1,0:T(8,128)(2,1)S(1)}, bf16[4,128,256]{2,1,0:T(8,128)(2,1)S(1)}, u32[]{:S(2)}, u32[]{:S(2)}) %collective-permute-start.3) | collective-permute-done | bytes 262176 | tf_op jit(solution)/shard_map/ppermute | solution.py:53
  28.7 1.6 %collective-permute-start.4 = (bf16[256,256]{1,0:T(8,128)(2,1)S(1)}, bf16[256,256]{1,0:T(8,128)(2,1)S(1)}, u32[]{:S(2)}, u32[]{:S(2)}) collective-permute-start(bf16[256,256]{1,0:T(8,128)(2,1)S(1)} %get-tuple-element.88), channel_id=1, source_target_pairs={{0,4},{4,0},{8,12},{12,8},{16,20},{20,16},{24,28},{28,24},{1,5},{5... | collective-permute-start | bytes 393224 | tf_op jit(solution)/shard_map/ppermute | solution.py:53
  30.9 1.4 %collective-permute-start.6 = (bf16[256,256]{1,0:T(8,128)(2,1)S(1)}, bf16[256,256]{1,0:T(8,128)(2,1)S(1)}, u32[]{:S(2)}, u32[]{:S(2)}) collective-permute-start(bf16[256,256]{1,0:T(8,128)(2,1)S(1)} %get-tuple-element.90), channel_id=1, source_target_pairs={{0,12},{4,8},{8,4},{12,0},{16,28},{20,24},{24,20},{28,16},{1,13},{... | collective-permute-start | bytes 393224 | tf_op jit(solution)/shard_map/ppermute | solution.py:53
  32.3 1.7 %add_near.1.local = f32[8,128,256]{2,1,0:T(8,128)S(1)} custom-call(s32[342]{0:T(512)S(1)} %concatenate.4.tab, bf16[16,128,128]{2,1,0:T(8,128)(2,1)S(1)} %copy-done.1, f32[8,128,256]{2,1,0:T(8,128)S(1)} %local_sum.1.local, bf16[4,128,256]{2,1,0:T(8,128)(2,1)S(1)} %collective-permute-done.3.offered.mirrored, ...), custom_call_target="tpu_custom_call" | custom-call | flops 67108864 | bytes 2097152 | tf_op jit(solution)/shard_map/add_near/pallas_call | solution.py:453
  34.1 1.9 %collective-permute-done.5.refs_1_ = bf16[256,256]{1,0:T(8,128)(2,1)S(1)} collective-permute-done((bf16[256,256]{1,0:T(8,128)(2,1)S(1)}, bf16[256,256]{1,0:T(8,128)(2,1)S(1)}, u32[]{:S(2)}, u32[]{:S(2)}) %collective-permute-start.5) | collective-permute-done | bytes 131104 | tf_op jit(solution)/shard_map/ppermute | solution.py:53
  36.0 2.0 %collective-permute-done.6.refs_0_ = bf16[256,256]{1,0:T(8,128)(2,1)S(1)} collective-permute-done((bf16[256,256]{1,0:T(8,128)(2,1)S(1)}, bf16[256,256]{1,0:T(8,128)(2,1)S(1)}, u32[]{:S(2)}, u32[]{:S(2)}) %collective-permute-start.6) | collective-permute-done | bytes 131104 | tf_op jit(solution)/shard_map/ppermute | solution.py:53
  39.4 1.7 %collective-permute-start.11 = (bf16[256,256]{1,0:T(8,128)(2,1)S(1)}, bf16[256,256]{1,0:T(8,128)(2,1)S(1)}, u32[]{:S(2)}, u32[]{:S(2)}) collective-permute-start(bf16[256,256]{1,0:T(8,128)(2,1)S(1)} %get-tuple-element.101), channel_id=1, source_target_pairs={{0,2},{1,3},{2,0},{3,1},{4,6},{5,7},{6,4},{7,5},{8,10},{9,11},{10,... | collective-permute-start | bytes 393224 | tf_op jit(solution)/shard_map/ppermute | solution.py:53
  41.2 4.5 %collective-permute-done.11.refs_2_ = bf16[256,256]{1,0:T(8,128)(2,1)S(1)} collective-permute-done((bf16[256,256]{1,0:T(8,128)(2,1)S(1)}, bf16[256,256]{1,0:T(8,128)(2,1)S(1)}, u32[]{:S(2)}, u32[]{:S(2)}) %collective-permute-start.11) | collective-permute-done | bytes 131104 | tf_op jit(solution)/shard_map/ppermute | solution.py:53
  45.7 1.9 %collective-permute-done.12.refs_3_ = bf16[256,256]{1,0:T(8,128)(2,1)S(1)} collective-permute-done((bf16[256,256]{1,0:T(8,128)(2,1)S(1)}, bf16[256,256]{1,0:T(8,128)(2,1)S(1)}, u32[]{:S(2)}, u32[]{:S(2)}) %collective-permute-start.12) | collective-permute-done | bytes 131104 | tf_op jit(solution)/shard_map/ppermute | solution.py:53
  49.8 1.7 %collective-permute-start.15 = (bf16[256,128]{1,0:T(8,128)(2,1)S(1)}, bf16[256,128]{1,0:T(8,128)(2,1)S(1)}, u32[]{:S(2)}, u32[]{:S(2)}) collective-permute-start(bf16[256,128]{1,0:T(8,128)(2,1)S(1)} %get-tuple-element.107), channel_id=1, source_target_pairs={{0,2},{1,3},{2,0},{3,1},{4,6},{5,7},{6,4},{7,5},{8,10},{9,11},{10,... | collective-permute-start | bytes 196616 | tf_op jit(solution)/shard_map/ppermute | solution.py:53
  52.1 1.9 %collective-permute-done.15.refs_2_ = bf16[256,128]{1,0:T(8,128)(2,1)S(1)} collective-permute-done((bf16[256,128]{1,0:T(8,128)(2,1)S(1)}, bf16[256,128]{1,0:T(8,128)(2,1)S(1)}, u32[]{:S(2)}, u32[]{:S(2)}) %collective-permute-start.15) | collective-permute-done | bytes 65568 | tf_op jit(solution)/shard_map/ppermute | solution.py:53
  54.0 1.6 %collective-permute-done.16.refs_3_ = bf16[256,128]{1,0:T(8,128)(2,1)S(1)} collective-permute-done((bf16[256,128]{1,0:T(8,128)(2,1)S(1)}, bf16[256,128]{1,0:T(8,128)(2,1)S(1)}, u32[]{:S(2)}, u32[]{:S(2)}) %collective-permute-start.16) | collective-permute-done | bytes 65568 | tf_op jit(solution)/shard_map/ppermute | solution.py:53
  58.6 1.4 %collective-permute-start.22 = (bf16[528,128]{1,0:T(8,128)(2,1)S(1)}, bf16[528,128]{1,0:T(8,128)(2,1)S(1)}, u32[]{:S(2)}, u32[]{:S(2)}) collective-permute-start(bf16[528,128]{1,0:T(8,128)(2,1)S(1)} %get-tuple-element.129), channel_id=1, source_target_pairs={{0,8},{4,12},{8,0},{12,4},{16,24},{20,28},{24,16},{28,20},{1,9},{5... | collective-permute-start | bytes 405512 | tf_op jit(solution)/shard_map/ppermute | solution.py:53
  61.3 2.2 %collective-permute-done.18.refs_0_ = bf16[528,128]{1,0:T(8,128)(2,1)S(1)} collective-permute-done((bf16[528,128]{1,0:T(8,128)(2,1)S(1)}, bf16[528,128]{1,0:T(8,128)(2,1)S(1)}, u32[]{:S(2)}, u32[]{:S(2)}) %collective-permute-start.18) | collective-permute-done | bytes 135200 | tf_op jit(solution)/shard_map/ppermute | solution.py:53
  69.1 2.4 %collective-permute-start.28 = (bf16[528,128]{1,0:T(8,128)(2,1)S(1)}, bf16[528,128]{1,0:T(8,128)(2,1)S(1)}, u32[]{:S(2)}, u32[]{:S(2)}) collective-permute-start(bf16[528,128]{1,0:T(8,128)(2,1)S(1)} %sum_mirror.1), channel_id=1, source_target_pairs={{0,16},{4,20},{8,24},{12,28},{16,0},{20,4},{24,8},{28,12},{1,17},{... | collective-permute-start | bytes 405512 | tf_op jit(solution)/shard_map/ppermute | solution.py:53
  71.5 2.2 %collective-permute-done.21.refs_0_ = bf16[2,32,512]{2,1,0:T(8,128)(2,1)S(1)} collective-permute-done((bf16[2,32,512]{2,1,0:T(8,128)(2,1)S(1)}, bf16[2,32,512]{2,1,0:T(8,128)(2,1)S(1)}, u32[]{:S(2)}, u32[]{:S(2)}) %collective-permute-start.21) | collective-permute-done | bytes 65568 | tf_op jit(solution)/shard_map/ppermute | solution.py:53
  73.7 2.3 %collective-permute-start.24 = (bf16[2,32,512]{2,1,0:T(8,128)(2,1)S(1)}, bf16[2,32,512]{2,1,0:T(8,128)(2,1)S(1)}, u32[]{:S(2)}, u32[]{:S(2)}) collective-permute-start(bf16[2,32,512]{2,1,0:T(8,128)(2,1)S(1)} %sum_half.1.here), channel_id=1, source_target_pairs={{0,16},{4,20},{8,24},{12,28},{16,0},{20,4},{24,8},{28,12},{1,17},{... | collective-permute-start | bytes 196616 | tf_op jit(solution)/shard_map/ppermute | solution.py:53
  75.9 3.0 %back_local.1.local = f32[8,128,128]{2,1,0:T(8,128)S(1)} custom-call(s32[342]{0:T(512)S(1)} %concatenate.4.tab, bf16[16,128,128]{2,1,0:T(8,128)(2,1)S(1)} %bitcast.8, bf16[8,128,128]{2,1,0:T(8,128)(2,1)S(1)} %get-tuple-element.138.own), custom_call_target="tpu_custom_call" | custom-call | flops 536870912 | bytes 786432 | tf_op jit(solution)/shard_map/back_local/pallas_call | solution.py:561
  81.8 1.6 %collective-permute-start.30 = (bf16[272,128]{1,0:T(8,128)(2,1)S(1)}, bf16[272,128]{1,0:T(8,128)(2,1)S(1)}, u32[]{:S(2)}, u32[]{:S(2)}) collective-permute-start(bf16[272,128]{1,0:T(8,128)(2,1)S(1)} %get-tuple-element.143), channel_id=1, source_target_pairs={{0,2},{1,3},{2,0},{3,1},{4,6},{5,7},{6,4},{7,5},{8,10},{9,11},{10,... | collective-permute-start | bytes 208904 | tf_op jit(solution)/shard_map/ppermute | solution.py:53
  84.4 1.6 %collective-permute-start.27 = (bf16[2,32,512]{2,1,0:T(8,128)(2,1)S(1)}, bf16[2,32,512]{2,1,0:T(8,128)(2,1)S(1)}, u32[]{:S(2)}, u32[]{:S(2)}) collective-permute-start(bf16[2,32,512]{2,1,0:T(8,128)(2,1)S(1)} %sum_both.1.refs_0_), channel_id=1, source_target_pairs={{0,12},{4,8},{8,4},{12,0},{16,28},{20,24},{24,20},{28,16},{1,13},{... | collective-permute-start | bytes 196616 | tf_op jit(solution)/shard_map/ppermute | solution.py:53
  86.0 2.5 %collective-permute-done.26.refs_2_ = bf16[2,32,512]{2,1,0:T(8,128)(2,1)S(1)} collective-permute-done((bf16[2,32,512]{2,1,0:T(8,128)(2,1)S(1)}, bf16[2,32,512]{2,1,0:T(8,128)(2,1)S(1)}, u32[]{:S(2)}, u32[]{:S(2)}) %collective-permute-start.26) | collective-permute-done | bytes 65568 | tf_op jit(solution)/shard_map/ppermute | solution.py:53
  90.4 1.6 %collective-permute-start.32 = (bf16[256,512]{1,0:T(8,128)(2,1)S(1)}, bf16[256,512]{1,0:T(8,128)(2,1)S(1)}, u32[]{:S(2)}, u32[]{:S(2)}) collective-permute-start(bf16[256,512]{1,0:T(8,128)(2,1)S(1)} %bitcast.10), channel_id=1, source_target_pairs={{0,2},{1,3},{2,0},{3,1},{4,6},{5,7},{6,4},{7,5},{8,10},{9,11},{10,... | collective-permute-start | bytes 786440 | tf_op jit(solution)/shard_map/ppermute | solution.py:53
  92.0 1.8 %node_grads.1 = (bf16[256,1024]{1,0:T(8,128)(2,1)}, f32[1,512]{1,0:T(1,128)}) custom-call(s32[2]{0:T(128)S(1)} %pad_add_fusion.ids, bf16[1024,512]{1,0:T(8,128)(2,1)S(1)} %copy-done.2, bf16[272,128]{1,0:T(8,128)(2,1)S(1)} %get-tuple-element.149.refs_0_, bf16[272,128]{1,0:T(8,128)(2,1)S(1)} %collective-permute-done.29.refs_1_, ...), custom_call_target="tpu_custom_call" | custom-call | flops 268435456 | bytes 1835008 | tf_op jit(solution)/shard_map/node_grads/pallas_call | solution.py:588
  93.8 1.6 %place_weight.3.refs_1_ = f32[1024,512]{1,0:T(8,128)} custom-call(s32[2]{0:T(128)S(1)} %pad_add_fusion.ids, bf16[256,512]{1,0:T(8,128)(2,1)S(1)} %bitcast.11, bf16[256,512]{1,0:T(8,128)(2,1)S(1)} %collective-permute-done.33.refs_1_), custom_call_target="tpu_custom_call" | custom-call | bytes 1572864 | tf_op jit(solution)/shard_map/place_weight/pallas_call | solution.py:607
  95.4 3.7 %collective-permute-done.32.refs_0_ = bf16[256,512]{1,0:T(8,128)(2,1)S(1)} collective-permute-done((bf16[256,512]{1,0:T(8,128)(2,1)S(1)}, bf16[256,512]{1,0:T(8,128)(2,1)S(1)}, u32[]{:S(2)}, u32[]{:S(2)}) %collective-permute-start.32) | collective-permute-done | bytes 262176 | tf_op jit(solution)/shard_map/ppermute | solution.py:53
  99.1 1.4 %place_weight.4.refs_1_ = f32[1024,512]{1,0:T(8,128)} custom-call(s32[2]{0:T(128)S(1)} %pad_add_fusion.ids, bf16[256,512]{1,0:T(8,128)(2,1)S(1)} %collective-permute-done.32.refs_0_, f32[1024,512]{1,0:T(8,128)} %place_weight.3.refs_1_), custom_call_target="tpu_custom_call", output_to_operand_aliasing={{}: (2, {})} | custom-call | bytes 1572864 | tf_op jit(solution)/shard_map/place_weight/pallas_call | solution.py:607
  100.6 1.4 %place_weight.5 = f32[1024,512]{1,0:T(8,128)} custom-call(s32[2]{0:T(128)S(1)} %pad_add_fusion.ids, bf16[256,512]{1,0:T(8,128)(2,1)S(1)} %collective-permute-done.34.refs_0_, f32[1024,512]{1,0:T(8,128)} %place_weight.4.refs_1_), custom_call_target="tpu_custom_call", output_to_operand_aliasing={{}: (2, {})} | custom-call | bytes 1572864 | tf_op jit(solution)/shard_map/place_weight/pallas_call | solution.py:607
  (88 shorter events, 31.8 us)
Async XLA Ops:
  2.4 9.2 %collective-permute-start = (bf16[256,256]{1,0:T(8,128)(2,1)S(1)}, bf16[256,256]{1,0:T(8,128)(2,1)S(1)}, u32[]{:S(2)}, u32[]{:S(2)}) collective-permute-start(bf16[256,256]{1,0:T(8,128)(2,1)S(1)} %get-tuple-element.81), channel_id=1, source_target_pairs={{0,3},{1,2},{2,1},{3,0},{4,7},{5,6},{6,5},{7,4},{8,11},{9,10},{10,... | collective-permute-start | bytes 393224 | tf_op jit(solution)/shard_map/ppermute | solution.py:53
  4.9 6.9 %collective-permute-start.1 = (bf16[256,256]{1,0:T(8,128)(2,1)S(1)}, bf16[256,256]{1,0:T(8,128)(2,1)S(1)}, u32[]{:S(2)}, u32[]{:S(2)}) collective-permute-start(bf16[256,256]{1,0:T(8,128)(2,1)S(1)} %get-tuple-element.82), channel_id=1, source_target_pairs={{0,2},{1,3},{2,0},{3,1},{4,6},{5,7},{6,4},{7,5},{8,10},{9,11},{10,... | collective-permute-start | bytes 393224 | tf_op jit(solution)/shard_map/ppermute | solution.py:53
  5.5 6.2 %collective-permute-start.2 = (bf16[256,256]{1,0:T(8,128)(2,1)S(1)}, bf16[256,256]{1,0:T(8,128)(2,1)S(1)}, u32[]{:S(2)}, u32[]{:S(2)}) collective-permute-start(bf16[256,256]{1,0:T(8,128)(2,1)S(1)} %get-tuple-element.83), channel_id=1, source_target_pairs={{0,1},{1,0},{2,3},{3,2},{4,5},{5,4},{6,7},{7,6},{8,9},{9,8},{10,11... | collective-permute-start | bytes 393224 | tf_op jit(solution)/shard_map/ppermute | solution.py:53
  12.4 15.7 %collective-permute-start.3 = (bf16[4,128,256]{2,1,0:T(8,128)(2,1)S(1)}, bf16[4,128,256]{2,1,0:T(8,128)(2,1)S(1)}, u32[]{:S(2)}, u32[]{:S(2)}) collective-permute-start(bf16[4,128,256]{2,1,0:T(8,128)(2,1)S(1)} %get-tuple-element.85), channel_id=1, source_target_pairs={{0,16},{4,20},{8,24},{12,28},{16,0},{20,4},{24,8},{28,12},{1,17},{... | collective-permute-start | bytes 786440 | tf_op jit(solution)/shard_map/ppermute | solution.py:53
  15.9 15.0 %collective-permute-start.7 = (bf16[256,256]{1,0:T(8,128)(2,1)S(1)}, bf16[256,256]{1,0:T(8,128)(2,1)S(1)}, u32[]{:S(2)}, u32[]{:S(2)}) collective-permute-start(bf16[256,256]{1,0:T(8,128)(2,1)S(1)} %get-tuple-element.92), channel_id=1, source_target_pairs={{0,4},{4,0},{8,12},{12,8},{16,20},{20,16},{24,28},{28,24},{1,5},{5... | collective-permute-start | bytes 393224 | tf_op jit(solution)/shard_map/ppermute | solution.py:53
  17.3 15.0 %collective-permute-start.8 = (bf16[256,256]{1,0:T(8,128)(2,1)S(1)}, bf16[256,256]{1,0:T(8,128)(2,1)S(1)}, u32[]{:S(2)}, u32[]{:S(2)}) collective-permute-start(bf16[256,256]{1,0:T(8,128)(2,1)S(1)} %get-tuple-element.93), channel_id=1, source_target_pairs={{0,8},{4,12},{8,0},{12,4},{16,24},{20,28},{24,16},{28,20},{1,9},{5... | collective-permute-start | bytes 393224 | tf_op jit(solution)/shard_map/ppermute | solution.py:53
  18.9 13.4 %collective-permute-start.9 = (bf16[256,256]{1,0:T(8,128)(2,1)S(1)}, bf16[256,256]{1,0:T(8,128)(2,1)S(1)}, u32[]{:S(2)}, u32[]{:S(2)}) collective-permute-start(bf16[256,256]{1,0:T(8,128)(2,1)S(1)} %get-tuple-element.94), channel_id=1, source_target_pairs={{0,12},{4,8},{8,4},{12,0},{16,28},{20,24},{24,20},{28,16},{1,13},{... | collective-permute-start | bytes 393224 | tf_op jit(solution)/shard_map/ppermute | solution.py:53
  28.7 5.4 %collective-permute-start.4 = (bf16[256,256]{1,0:T(8,128)(2,1)S(1)}, bf16[256,256]{1,0:T(8,128)(2,1)S(1)}, u32[]{:S(2)}, u32[]{:S(2)}) collective-permute-start(bf16[256,256]{1,0:T(8,128)(2,1)S(1)} %get-tuple-element.88), channel_id=1, source_target_pairs={{0,4},{4,0},{8,12},{12,8},{16,20},{20,16},{24,28},{28,24},{1,5},{5... | collective-permute-start | bytes 393224 | tf_op jit(solution)/shard_map/ppermute | solution.py:53
  30.3 5.7 %collective-permute-start.5 = (bf16[256,256]{1,0:T(8,128)(2,1)S(1)}, bf16[256,256]{1,0:T(8,128)(2,1)S(1)}, u32[]{:S(2)}, u32[]{:S(2)}) collective-permute-start(bf16[256,256]{1,0:T(8,128)(2,1)S(1)} %get-tuple-element.89), channel_id=1, source_target_pairs={{0,8},{4,12},{8,0},{12,4},{16,24},{20,28},{24,16},{28,20},{1,9},{5... | collective-permute-start | bytes 393224 | tf_op jit(solution)/shard_map/ppermute | solution.py:53
  30.9 7.1 %collective-permute-start.6 = (bf16[256,256]{1,0:T(8,128)(2,1)S(1)}, bf16[256,256]{1,0:T(8,128)(2,1)S(1)}, u32[]{:S(2)}, u32[]{:S(2)}) collective-permute-start(bf16[256,256]{1,0:T(8,128)(2,1)S(1)} %get-tuple-element.90), channel_id=1, source_target_pairs={{0,12},{4,8},{8,4},{12,0},{16,28},{20,24},{24,20},{28,16},{1,13},{... | collective-permute-start | bytes 393224 | tf_op jit(solution)/shard_map/ppermute | solution.py:53
  39.4 6.4 %collective-permute-start.11 = (bf16[256,256]{1,0:T(8,128)(2,1)S(1)}, bf16[256,256]{1,0:T(8,128)(2,1)S(1)}, u32[]{:S(2)}, u32[]{:S(2)}) collective-permute-start(bf16[256,256]{1,0:T(8,128)(2,1)S(1)} %get-tuple-element.101), channel_id=1, source_target_pairs={{0,2},{1,3},{2,0},{3,1},{4,6},{5,7},{6,4},{7,5},{8,10},{9,11},{10,... | collective-permute-start | bytes 393224 | tf_op jit(solution)/shard_map/ppermute | solution.py:53
  41.1 6.6 %collective-permute-start.12 = (bf16[256,256]{1,0:T(8,128)(2,1)S(1)}, bf16[256,256]{1,0:T(8,128)(2,1)S(1)}, u32[]{:S(2)}, u32[]{:S(2)}) collective-permute-start(bf16[256,256]{1,0:T(8,128)(2,1)S(1)} %get-tuple-element.102), channel_id=1, source_target_pairs={{0,3},{1,2},{2,1},{3,0},{4,7},{5,6},{6,5},{7,4},{8,11},{9,10},{10,... | collective-permute-start | bytes 393224 | tf_op jit(solution)/shard_map/ppermute | solution.py:53
  49.2 6.5 %collective-permute-start.13 = (bf16[2,256,512]{2,1,0:T(8,128)(2,1)S(1)}, bf16[2,256,512]{2,1,0:T(8,128)(2,1)S(1)}, u32[]{:S(2)}, u32[]{:S(2)}) collective-permute-start(bf16[2,256,512]{2,1,0:T(8,128)(2,1)S(1)} %get-tuple-element.104), channel_id=1, source_target_pairs={{0,1},{1,0},{2,3},{3,2},{4,5},{5,4},{6,7},{7,6},{8,9},{9,8},{10,11... | collective-permute-start | bytes 1572872 | tf_op jit(solution)/shard_map/ppermute | solution.py:53
  49.8 4.3 %collective-permute-start.15 = (bf16[256,128]{1,0:T(8,128)(2,1)S(1)}, bf16[256,128]{1,0:T(8,128)(2,1)S(1)}, u32[]{:S(2)}, u32[]{:S(2)}) collective-permute-start(bf16[256,128]{1,0:T(8,128)(2,1)S(1)} %get-tuple-element.107), channel_id=1, source_target_pairs={{0,2},{1,3},{2,0},{3,1},{4,6},{5,7},{6,4},{7,5},{8,10},{9,11},{10,... | collective-permute-start | bytes 196616 | tf_op jit(solution)/shard_map/ppermute | solution.py:53
  51.4 4.2 %collective-permute-start.16 = (bf16[256,128]{1,0:T(8,128)(2,1)S(1)}, bf16[256,128]{1,0:T(8,128)(2,1)S(1)}, u32[]{:S(2)}, u32[]{:S(2)}) collective-permute-start(bf16[256,128]{1,0:T(8,128)(2,1)S(1)} %get-tuple-element.108), channel_id=1, source_target_pairs={{0,3},{1,2},{2,1},{3,0},{4,7},{5,6},{6,5},{7,4},{8,11},{9,10},{10,... | collective-permute-start | bytes 196616 | tf_op jit(solution)/shard_map/ppermute | solution.py:53
  55.8 8.4 %collective-permute-start.17 = (bf16[1,256,512]{2,1,0:T(8,128)(2,1)S(1)}, bf16[1,256,512]{2,1,0:T(8,128)(2,1)S(1)}, u32[]{:S(2)}, u32[]{:S(2)}) collective-permute-start(bf16[1,256,512]{2,1,0:T(8,128)(2,1)S(1)} %get-tuple-element.114), channel_id=1, source_target_pairs={{0,2},{1,3},{2,0},{3,1},{4,6},{5,7},{6,4},{7,5},{8,10},{9,11},{10,... | collective-permute-start | bytes 786440 | tf_op jit(solution)/shard_map/ppermute | solution.py:53
  57.7 5.8 %collective-permute-start.18 = (bf16[528,128]{1,0:T(8,128)(2,1)S(1)}, bf16[528,128]{1,0:T(8,128)(2,1)S(1)}, u32[]{:S(2)}, u32[]{:S(2)}) collective-permute-start(bf16[528,128]{1,0:T(8,128)(2,1)S(1)} %get-tuple-element.120), channel_id=1, source_target_pairs={{0,4},{4,0},{8,12},{12,8},{16,20},{20,16},{24,28},{28,24},{1,5},{5... | collective-permute-start | bytes 405512 | tf_op jit(solution)/shard_map/ppermute | solution.py:53
  58.6 9.7 %collective-permute-start.22 = (bf16[528,128]{1,0:T(8,128)(2,1)S(1)}, bf16[528,128]{1,0:T(8,128)(2,1)S(1)}, u32[]{:S(2)}, u32[]{:S(2)}) collective-permute-start(bf16[528,128]{1,0:T(8,128)(2,1)S(1)} %get-tuple-element.129), channel_id=1, source_target_pairs={{0,8},{4,12},{8,0},{12,4},{16,24},{20,28},{24,16},{28,20},{1,9},{5... | collective-permute-start | bytes 405512 | tf_op jit(solution)/shard_map/ppermute | solution.py:53
  60.1 8.3 %collective-permute-start.23 = (bf16[528,128]{1,0:T(8,128)(2,1)S(1)}, bf16[528,128]{1,0:T(8,128)(2,1)S(1)}, u32[]{:S(2)}, u32[]{:S(2)}) collective-permute-start(bf16[528,128]{1,0:T(8,128)(2,1)S(1)} %get-tuple-element.130), channel_id=1, source_target_pairs={{0,12},{4,8},{8,4},{12,0},{16,28},{20,24},{24,20},{28,16},{1,13},{... | collective-permute-start | bytes 405512 | tf_op jit(solution)/shard_map/ppermute | solution.py:53
  64.8 6.7 %collective-permute-start.19 = (bf16[2,32,512]{2,1,0:T(8,128)(2,1)S(1)}, bf16[2,32,512]{2,1,0:T(8,128)(2,1)S(1)}, u32[]{:S(2)}, u32[]{:S(2)}) collective-permute-start(bf16[2,32,512]{2,1,0:T(8,128)(2,1)S(1)} %get-tuple-element.123), channel_id=1, source_target_pairs={{0,4},{4,0},{8,12},{12,8},{16,20},{20,16},{24,28},{28,24},{1,5},{5... | collective-permute-start | bytes 196616 | tf_op jit(solution)/shard_map/ppermute | solution.py:53
  65.7 5.8 %collective-permute-start.20 = (bf16[2,32,512]{2,1,0:T(8,128)(2,1)S(1)}, bf16[2,32,512]{2,1,0:T(8,128)(2,1)S(1)}, u32[]{:S(2)}, u32[]{:S(2)}) collective-permute-start(bf16[2,32,512]{2,1,0:T(8,128)(2,1)S(1)} %get-tuple-element.124), channel_id=1, source_target_pairs={{0,8},{4,12},{8,0},{12,4},{16,24},{20,28},{24,16},{28,20},{1,9},{5... | collective-permute-start | bytes 196616 | tf_op jit(solution)/shard_map/ppermute | solution.py:53
  67.0 6.6 %collective-permute-start.21 = (bf16[2,32,512]{2,1,0:T(8,128)(2,1)S(1)}, bf16[2,32,512]{2,1,0:T(8,128)(2,1)S(1)}, u32[]{:S(2)}, u32[]{:S(2)}) collective-permute-start(bf16[2,32,512]{2,1,0:T(8,128)(2,1)S(1)} %get-tuple-element.125), channel_id=1, source_target_pairs={{0,12},{4,8},{8,4},{12,0},{16,28},{20,24},{24,20},{28,16},{1,13},{... | collective-permute-start | bytes 196616 | tf_op jit(solution)/shard_map/ppermute | solution.py:53
  69.1 11.9 %collective-permute-start.28 = (bf16[528,128]{1,0:T(8,128)(2,1)S(1)}, bf16[528,128]{1,0:T(8,128)(2,1)S(1)}, u32[]{:S(2)}, u32[]{:S(2)}) collective-permute-start(bf16[528,128]{1,0:T(8,128)(2,1)S(1)} %sum_mirror.1), channel_id=1, source_target_pairs={{0,16},{4,20},{8,24},{12,28},{16,0},{20,4},{24,8},{28,12},{1,17},{... | collective-permute-start | bytes 405512 | tf_op jit(solution)/shard_map/ppermute | solution.py:53
  73.7 6.0 %collective-permute-start.24 = (bf16[2,32,512]{2,1,0:T(8,128)(2,1)S(1)}, bf16[2,32,512]{2,1,0:T(8,128)(2,1)S(1)}, u32[]{:S(2)}, u32[]{:S(2)}) collective-permute-start(bf16[2,32,512]{2,1,0:T(8,128)(2,1)S(1)} %sum_half.1.here), channel_id=1, source_target_pairs={{0,16},{4,20},{8,24},{12,28},{16,0},{20,4},{24,8},{28,12},{1,17},{... | collective-permute-start | bytes 196616 | tf_op jit(solution)/shard_map/ppermute | solution.py:53
  79.7 4.6 %collective-permute-start.25 = (bf16[2,32,512]{2,1,0:T(8,128)(2,1)S(1)}, bf16[2,32,512]{2,1,0:T(8,128)(2,1)S(1)}, u32[]{:S(2)}, u32[]{:S(2)}) collective-permute-start(bf16[2,32,512]{2,1,0:T(8,128)(2,1)S(1)} %sum_both.1.refs_0_), channel_id=1, source_target_pairs={{0,4},{4,0},{8,12},{12,8},{16,20},{20,16},{24,28},{28,24},{1,5},{5... | collective-permute-start | bytes 196616 | tf_op jit(solution)/shard_map/ppermute | solution.py:53
  81.7 8.0 %collective-permute-start.29 = (bf16[272,128]{1,0:T(8,128)(2,1)S(1)}, bf16[272,128]{1,0:T(8,128)(2,1)S(1)}, u32[]{:S(2)}, u32[]{:S(2)}) collective-permute-start(bf16[272,128]{1,0:T(8,128)(2,1)S(1)} %get-tuple-element.142), channel_id=1, source_target_pairs={{0,1},{1,0},{2,3},{3,2},{4,5},{5,4},{6,7},{7,6},{8,9},{9,8},{10,11... | collective-permute-start | bytes 208904 | tf_op jit(solution)/shard_map/ppermute | solution.py:53
  81.8 7.9 %collective-permute-start.30 = (bf16[272,128]{1,0:T(8,128)(2,1)S(1)}, bf16[272,128]{1,0:T(8,128)(2,1)S(1)}, u32[]{:S(2)}, u32[]{:S(2)}) collective-permute-start(bf16[272,128]{1,0:T(8,128)(2,1)S(1)} %get-tuple-element.143), channel_id=1, source_target_pairs={{0,2},{1,3},{2,0},{3,1},{4,6},{5,7},{6,4},{7,5},{8,10},{9,11},{10,... | collective-permute-start | bytes 208904 | tf_op jit(solution)/shard_map/ppermute | solution.py:53
  83.4 6.3 %collective-permute-start.31 = (bf16[272,128]{1,0:T(8,128)(2,1)S(1)}, bf16[272,128]{1,0:T(8,128)(2,1)S(1)}, u32[]{:S(2)}, u32[]{:S(2)}) collective-permute-start(bf16[272,128]{1,0:T(8,128)(2,1)S(1)} %get-tuple-element.144), channel_id=1, source_target_pairs={{0,3},{1,2},{2,1},{3,0},{4,7},{5,6},{6,5},{7,4},{8,11},{9,10},{10,... | collective-permute-start | bytes 208904 | tf_op jit(solution)/shard_map/ppermute | solution.py:53
  83.6 4.9 %collective-permute-start.26 = (bf16[2,32,512]{2,1,0:T(8,128)(2,1)S(1)}, bf16[2,32,512]{2,1,0:T(8,128)(2,1)S(1)}, u32[]{:S(2)}, u32[]{:S(2)}) collective-permute-start(bf16[2,32,512]{2,1,0:T(8,128)(2,1)S(1)} %sum_both.1.refs_0_), channel_id=1, source_target_pairs={{0,8},{4,12},{8,0},{12,4},{16,24},{20,28},{24,16},{28,20},{1,9},{5... | collective-permute-start | bytes 196616 | tf_op jit(solution)/shard_map/ppermute | solution.py:53
  84.4 5.3 %collective-permute-start.27 = (bf16[2,32,512]{2,1,0:T(8,128)(2,1)S(1)}, bf16[2,32,512]{2,1,0:T(8,128)(2,1)S(1)}, u32[]{:S(2)}, u32[]{:S(2)}) collective-permute-start(bf16[2,32,512]{2,1,0:T(8,128)(2,1)S(1)} %sum_both.1.refs_0_), channel_id=1, source_target_pairs={{0,12},{4,8},{8,4},{12,0},{16,28},{20,24},{24,20},{28,16},{1,13},{... | collective-permute-start | bytes 196616 | tf_op jit(solution)/shard_map/ppermute | solution.py:53
  90.3 3.5 %collective-permute-start.33 = (bf16[256,512]{1,0:T(8,128)(2,1)S(1)}, bf16[256,512]{1,0:T(8,128)(2,1)S(1)}, u32[]{:S(2)}, u32[]{:S(2)}) collective-permute-start(bf16[256,512]{1,0:T(8,128)(2,1)S(1)} %bitcast.9), channel_id=1, source_target_pairs={{0,1},{1,0},{2,3},{3,2},{4,5},{5,4},{6,7},{7,6},{8,9},{9,8},{10,11... | collective-permute-start | bytes 786440 | tf_op jit(solution)/shard_map/ppermute | solution.py:53
  90.4 8.7 %collective-permute-start.32 = (bf16[256,512]{1,0:T(8,128)(2,1)S(1)}, bf16[256,512]{1,0:T(8,128)(2,1)S(1)}, u32[]{:S(2)}, u32[]{:S(2)}) collective-permute-start(bf16[256,512]{1,0:T(8,128)(2,1)S(1)} %bitcast.10), channel_id=1, source_target_pairs={{0,2},{1,3},{2,0},{3,1},{4,6},{5,7},{6,4},{7,5},{8,10},{9,11},{10,... | collective-permute-start | bytes 786440 | tf_op jit(solution)/shard_map/ppermute | solution.py:53
  (9 other events, 70.5 us)

commit v2 on v0

--- a/solution.py
+++ b/solution.py
@@ -287,7 +287,7 @@
 
 def join_shares(ids, *refs):
     parts, out = refs[:-1], refs[-1]
-    for m, part in enumerate(parts):
+    for m, part in zip(reversed(range(len(parts))), parts):
         owner = jnp.bitwise_xor(ids[0], m)
         out[owner] = part[0]
         out[jnp.bitwise_xor(owner, len(parts))] = part[1]
@@ -600,7 +600,7 @@
         [SMEM] + [VMEM] * half,
         nbytes=4 * narrow * hidden,
         name="join_shares",
-    )(ids, *gathered).reshape(narrow, hidden)
+    )(ids, *reversed(gathered)).reshape(narrow, hidden)
     count = groups // 2
 
     def place(parts, masks, before=()):

time: 102 us -> 102 us (level)
  transfers between devices with their start and end apart: 35 -> 35, of which waited for: 17 -> 18; matrix products, arithmetic and copies ran while one was open for 6% -> 6% of each run, Pallas kernels for 16% -> 16%
where the time goes in v2:
time: 102 us
  starting transfers between devices  37.5 us (37%)
  waiting for transfers between devices  32.4 us (32%)
  Pallas kernels  23 us (23%)
  local copies, waits for them, and re-layouts  8.41 us (8%)
    ppermute x35, starting transfers between devices, swap(): lax.ppermute(value, axis, [(i, i ^ mask) for i in range(lax.axis_size(axi...  37.5 us
    ppermute x35, waiting for transfers between devices, swap(): lax.ppermute(value, axis, [(i, i ^ mask) for i in range(lax.axis_size(axi...  32.4 us
    pallas_call x3, Pallas kernels, place(): call(functools.partial(place_weight, masks), out_shape=shape((embed, hidd...  4.31 us
    unnamed x15, local copies, waits for them, and re-layouts  3.89 us
    pallas_call x1, Pallas kernels, per_device(): call(functools.partial(local_sum, per_row, at), shape((blocks, tile, narr...  3.07 us
    pallas_call x1, Pallas kernels, per_device(): call(functools.partial(back_local, per_row, at), shape((blocks, tile, wid...  2.98 us
  transfers between devices with their start and end apart: 35, of which 18 were waited for; matrix products, arithmetic and copies ran while one was open for 6% of the time, Pallas kernels for 16%

profile of v2, /device:TPU:0, one launch (start us, length us, event | category | flops | bytes accessed | tf_op | source)
XLA Modules:
  0.0 102.2 jit_solution(16372091536964003660)
XLA Ops:
  2.4 2.5 %collective-permute-start = (bf16[256,256]{1,0:T(8,128)(2,1)S(1)}, bf16[256,256]{1,0:T(8,128)(2,1)S(1)}, u32[]{:S(2)}, u32[]{:S(2)}) collective-permute-start(bf16[256,256]{1,0:T(8,128)(2,1)S(1)} %get-tuple-element.81), channel_id=1, source_target_pairs={{0,3},{1,2},{2,1},{3,0},{4,7},{5,6},{6,5},{7,4},{8,11},{9,10},{10,... | collective-permute-start | bytes 393224 | tf_op jit(solution)/shard_map/ppermute | solution.py:53
  12.4 3.4 %collective-permute-start.3 = (bf16[4,128,256]{2,1,0:T(8,128)(2,1)S(1)}, bf16[4,128,256]{2,1,0:T(8,128)(2,1)S(1)}, u32[]{:S(2)}, u32[]{:S(2)}) collective-permute-start(bf16[4,128,256]{2,1,0:T(8,128)(2,1)S(1)} %get-tuple-element.85), channel_id=1, source_target_pairs={{0,16},{4,20},{8,24},{12,28},{16,0},{20,4},{24,8},{28,12},{1,17},{... | collective-permute-start | bytes 786440 | tf_op jit(solution)/shard_map/ppermute | solution.py:53
  15.9 1.5 %collective-permute-start.7 = (bf16[256,256]{1,0:T(8,128)(2,1)S(1)}, bf16[256,256]{1,0:T(8,128)(2,1)S(1)}, u32[]{:S(2)}, u32[]{:S(2)}) collective-permute-start(bf16[256,256]{1,0:T(8,128)(2,1)S(1)} %get-tuple-element.92), channel_id=1, source_target_pairs={{0,4},{4,0},{8,12},{12,8},{16,20},{20,16},{24,28},{28,24},{1,5},{5... | collective-permute-start | bytes 393224 | tf_op jit(solution)/shard_map/ppermute | solution.py:53
  17.3 1.6 %collective-permute-start.8 = (bf16[256,256]{1,0:T(8,128)(2,1)S(1)}, bf16[256,256]{1,0:T(8,128)(2,1)S(1)}, u32[]{:S(2)}, u32[]{:S(2)}) collective-permute-start(bf16[256,256]{1,0:T(8,128)(2,1)S(1)} %get-tuple-element.93), channel_id=1, source_target_pairs={{0,8},{4,12},{8,0},{12,4},{16,24},{20,28},{24,16},{28,20},{1,9},{5... | collective-permute-start | bytes 393224 | tf_op jit(solution)/shard_map/ppermute | solution.py:53
  20.4 3.1 %local_sum.1.local = f32[8,128,256]{2,1,0:T(8,128)S(1)} custom-call(s32[342]{0:T(512)S(1)} %concatenate.4.tab, bf16[16,128,128]{2,1,0:T(8,128)(2,1)S(1)} %copy-done, bf16[8,128,256]{2,1,0:T(8,128)(2,1)S(1)} %get-tuple-element.86.x), custom_call_target="tpu_custom_call" | custom-call | flops 1073741824 | bytes 1572864 | tf_op jit(solution)/shard_map/local_sum/pallas_call | solution.py:436
  23.5 4.6 %collective-permute-done.3.offered.mirrored = bf16[4,128,256]{2,1,0:T(8,128)(2,1)S(1)} collective-permute-done((bf16[4,128,256]{2,1,0:T(8,128)(2,1)S(1)}, bf16[4,128,256]{2,1,0:T(8,128)(2,1)S(1)}, u32[]{:S(2)}, u32[]{:S(2)}) %collective-permute-start.3) | collective-permute-done | bytes 262176 | tf_op jit(solution)/shard_map/ppermute | solution.py:53
  28.7 1.6 %collective-permute-start.4 = (bf16[256,256]{1,0:T(8,128)(2,1)S(1)}, bf16[256,256]{1,0:T(8,128)(2,1)S(1)}, u32[]{:S(2)}, u32[]{:S(2)}) collective-permute-start(bf16[256,256]{1,0:T(8,128)(2,1)S(1)} %get-tuple-element.88), channel_id=1, source_target_pairs={{0,4},{4,0},{8,12},{12,8},{16,20},{20,16},{24,28},{28,24},{1,5},{5... | collective-permute-start | bytes 393224 | tf_op jit(solution)/shard_map/ppermute | solution.py:53
  30.9 1.4 %collective-permute-start.6 = (bf16[256,256]{1,0:T(8,128)(2,1)S(1)}, bf16[256,256]{1,0:T(8,128)(2,1)S(1)}, u32[]{:S(2)}, u32[]{:S(2)}) collective-permute-start(bf16[256,256]{1,0:T(8,128)(2,1)S(1)} %get-tuple-element.90), channel_id=1, source_target_pairs={{0,12},{4,8},{8,4},{12,0},{16,28},{20,24},{24,20},{28,16},{1,13},{... | collective-permute-start | bytes 393224 | tf_op jit(solution)/shard_map/ppermute | solution.py:53
  32.3 1.5 %add_near.1.local = f32[8,128,256]{2,1,0:T(8,128)S(1)} custom-call(s32[342]{0:T(512)S(1)} %concatenate.4.tab, bf16[16,128,128]{2,1,0:T(8,128)(2,1)S(1)} %copy-done.1, f32[8,128,256]{2,1,0:T(8,128)S(1)} %local_sum.1.local, bf16[4,128,256]{2,1,0:T(8,128)(2,1)S(1)} %collective-permute-done.3.offered.mirrored, ...), custom_call_target="tpu_custom_call" | custom-call | flops 67108864 | bytes 2097152 | tf_op jit(solution)/shard_map/add_near/pallas_call | solution.py:453
  34.1 1.9 %collective-permute-done.5.refs_1_ = bf16[256,256]{1,0:T(8,128)(2,1)S(1)} collective-permute-done((bf16[256,256]{1,0:T(8,128)(2,1)S(1)}, bf16[256,256]{1,0:T(8,128)(2,1)S(1)}, u32[]{:S(2)}, u32[]{:S(2)}) %collective-permute-start.5) | collective-permute-done | bytes 131104 | tf_op jit(solution)/shard_map/ppermute | solution.py:53
  36.0 2.0 %collective-permute-done.6.refs_2_ = bf16[256,256]{1,0:T(8,128)(2,1)S(1)} collective-permute-done((bf16[256,256]{1,0:T(8,128)(2,1)S(1)}, bf16[256,256]{1,0:T(8,128)(2,1)S(1)}, u32[]{:S(2)}, u32[]{:S(2)}) %collective-permute-start.6) | collective-permute-done | bytes 131104 | tf_op jit(solution)/shard_map/ppermute | solution.py:53
  38.0 1.4 %add_far.1 = (bf16[256,256]{1,0:T(8,128)(2,1)S(1)}, bf16[256,256]{1,0:T(8,128)(2,1)S(1)}, bf16[256,256]{1,0:T(8,128)(2,1)S(1)}, bf16[256,256]{1,0:T(8,128)(2,1)S(1)}) custom-call(s32[342]{0:T(512)S(1)} %concatenate.4.tab, bf16[16,128,128]{2,1,0:T(8,128)(2,1)S(1)} %copy-done.1, f32[8,128,256]{2,1,0:T(8,128)S(1)} %add_near.1.local, ...), custom_call_target="tpu_custom_call" | custom-call | flops 67108864 | bytes 2097152 | tf_op jit(solution)/shard_map/add_far/pallas_call | solution.py:462
  39.5 1.7 %collective-permute-start.11 = (bf16[256,256]{1,0:T(8,128)(2,1)S(1)}, bf16[256,256]{1,0:T(8,128)(2,1)S(1)}, u32[]{:S(2)}, u32[]{:S(2)}) collective-permute-start(bf16[256,256]{1,0:T(8,128)(2,1)S(1)} %get-tuple-element.101), channel_id=1, source_target_pairs={{0,2},{1,3},{2,0},{3,1},{4,6},{5,7},{6,4},{7,5},{8,10},{9,11},{10,... | collective-permute-start | bytes 393224 | tf_op jit(solution)/shard_map/ppermute | solution.py:53
  41.4 4.5 %collective-permute-done.11.refs_2_ = bf16[256,256]{1,0:T(8,128)(2,1)S(1)} collective-permute-done((bf16[256,256]{1,0:T(8,128)(2,1)S(1)}, bf16[256,256]{1,0:T(8,128)(2,1)S(1)}, u32[]{:S(2)}, u32[]{:S(2)}) %collective-permute-start.11) | collective-permute-done | bytes 131104 | tf_op jit(solution)/shard_map/ppermute | solution.py:53
  45.9 1.9 %collective-permute-done.12.refs_3_ = bf16[256,256]{1,0:T(8,128)(2,1)S(1)} collective-permute-done((bf16[256,256]{1,0:T(8,128)(2,1)S(1)}, bf16[256,256]{1,0:T(8,128)(2,1)S(1)}, u32[]{:S(2)}, u32[]{:S(2)}) %collective-permute-start.12) | collective-permute-done | bytes 131104 | tf_op jit(solution)/shard_map/ppermute | solution.py:53
  49.9 1.6 %collective-permute-start.15 = (bf16[256,128]{1,0:T(8,128)(2,1)S(1)}, bf16[256,128]{1,0:T(8,128)(2,1)S(1)}, u32[]{:S(2)}, u32[]{:S(2)}) collective-permute-start(bf16[256,128]{1,0:T(8,128)(2,1)S(1)} %get-tuple-element.107), channel_id=1, source_target_pairs={{0,2},{1,3},{2,0},{3,1},{4,6},{5,7},{6,4},{7,5},{8,10},{9,11},{10,... | collective-permute-start | bytes 196616 | tf_op jit(solution)/shard_map/ppermute | solution.py:53
  52.3 1.9 %collective-permute-done.15.refs_2_ = bf16[256,128]{1,0:T(8,128)(2,1)S(1)} collective-permute-done((bf16[256,128]{1,0:T(8,128)(2,1)S(1)}, bf16[256,128]{1,0:T(8,128)(2,1)S(1)}, u32[]{:S(2)}, u32[]{:S(2)}) %collective-permute-start.15) | collective-permute-done | bytes 65568 | tf_op jit(solution)/shard_map/ppermute | solution.py:53
  54.2 1.6 %collective-permute-done.16.refs_3_ = bf16[256,128]{1,0:T(8,128)(2,1)S(1)} collective-permute-done((bf16[256,128]{1,0:T(8,128)(2,1)S(1)}, bf16[256,128]{1,0:T(8,128)(2,1)S(1)}, u32[]{:S(2)}, u32[]{:S(2)}) %collective-permute-start.16) | collective-permute-done | bytes 65568 | tf_op jit(solution)/shard_map/ppermute | solution.py:53
  58.8 1.6 %collective-permute-start.22 = (bf16[528,128]{1,0:T(8,128)(2,1)S(1)}, bf16[528,128]{1,0:T(8,128)(2,1)S(1)}, u32[]{:S(2)}, u32[]{:S(2)}) collective-permute-start(bf16[528,128]{1,0:T(8,128)(2,1)S(1)} %get-tuple-element.129), channel_id=1, source_target_pairs={{0,8},{4,12},{8,0},{12,4},{16,24},{20,28},{24,16},{28,20},{1,9},{5... | collective-permute-start | bytes 405512 | tf_op jit(solution)/shard_map/ppermute | solution.py:53
  61.4 2.2 %collective-permute-done.18.refs_0_ = bf16[528,128]{1,0:T(8,128)(2,1)S(1)} collective-permute-done((bf16[528,128]{1,0:T(8,128)(2,1)S(1)}, bf16[528,128]{1,0:T(8,128)(2,1)S(1)}, u32[]{:S(2)}, u32[]{:S(2)}) %collective-permute-start.18) | collective-permute-done | bytes 135200 | tf_op jit(solution)/shard_map/ppermute | solution.py:53
  65.8 1.5 %collective-permute-start.20 = (bf16[2,32,512]{2,1,0:T(8,128)(2,1)S(1)}, bf16[2,32,512]{2,1,0:T(8,128)(2,1)S(1)}, u32[]{:S(2)}, u32[]{:S(2)}) collective-permute-start(bf16[2,32,512]{2,1,0:T(8,128)(2,1)S(1)} %get-tuple-element.124), channel_id=1, source_target_pairs={{0,8},{4,12},{8,0},{12,4},{16,24},{20,28},{24,16},{28,20},{1,9},{5... | collective-permute-start | bytes 196616 | tf_op jit(solution)/shard_map/ppermute | solution.py:53
  69.1 2.3 %collective-permute-start.28 = (bf16[528,128]{1,0:T(8,128)(2,1)S(1)}, bf16[528,128]{1,0:T(8,128)(2,1)S(1)}, u32[]{:S(2)}, u32[]{:S(2)}) collective-permute-start(bf16[528,128]{1,0:T(8,128)(2,1)S(1)} %sum_mirror.1), channel_id=1, source_target_pairs={{0,16},{4,20},{8,24},{12,28},{16,0},{20,4},{24,8},{28,12},{1,17},{... | collective-permute-start | bytes 405512 | tf_op jit(solution)/shard_map/ppermute | solution.py:53
  71.5 2.1 %collective-permute-done.21.refs_2_ = bf16[2,32,512]{2,1,0:T(8,128)(2,1)S(1)} collective-permute-done((bf16[2,32,512]{2,1,0:T(8,128)(2,1)S(1)}, bf16[2,32,512]{2,1,0:T(8,128)(2,1)S(1)}, u32[]{:S(2)}, u32[]{:S(2)}) %collective-permute-start.21) | collective-permute-done | bytes 65568 | tf_op jit(solution)/shard_map/ppermute | solution.py:53
  73.6 2.5 %collective-permute-start.24 = (bf16[2,32,512]{2,1,0:T(8,128)(2,1)S(1)}, bf16[2,32,512]{2,1,0:T(8,128)(2,1)S(1)}, u32[]{:S(2)}, u32[]{:S(2)}) collective-permute-start(bf16[2,32,512]{2,1,0:T(8,128)(2,1)S(1)} %sum_half.1.here), channel_id=1, source_target_pairs={{0,16},{4,20},{8,24},{12,28},{16,0},{20,4},{24,8},{28,12},{1,17},{... | collective-permute-start | bytes 196616 | tf_op jit(solution)/shard_map/ppermute | solution.py:53
  76.1 3.0 %back_local.1.local = f32[8,128,128]{2,1,0:T(8,128)S(1)} custom-call(s32[342]{0:T(512)S(1)} %concatenate.4.tab, bf16[16,128,128]{2,1,0:T(8,128)(2,1)S(1)} %bitcast.8, bf16[8,128,128]{2,1,0:T(8,128)(2,1)S(1)} %get-tuple-element.138.own), custom_call_target="tpu_custom_call" | custom-call | flops 536870912 | bytes 786432 | tf_op jit(solution)/shard_map/back_local/pallas_call | solution.py:561
  81.7 1.5 %collective-permute-start.30 = (bf16[272,128]{1,0:T(8,128)(2,1)S(1)}, bf16[272,128]{1,0:T(8,128)(2,1)S(1)}, u32[]{:S(2)}, u32[]{:S(2)}) collective-permute-start(bf16[272,128]{1,0:T(8,128)(2,1)S(1)} %get-tuple-element.143), channel_id=1, source_target_pairs={{0,2},{1,3},{2,0},{3,1},{4,6},{5,7},{6,4},{7,5},{8,10},{9,11},{10,... | collective-permute-start | bytes 208904 | tf_op jit(solution)/shard_map/ppermute | solution.py:53
  84.2 1.9 %collective-permute-start.27 = (bf16[2,32,512]{2,1,0:T(8,128)(2,1)S(1)}, bf16[2,32,512]{2,1,0:T(8,128)(2,1)S(1)}, u32[]{:S(2)}, u32[]{:S(2)}) collective-permute-start(bf16[2,32,512]{2,1,0:T(8,128)(2,1)S(1)} %sum_both.1.refs_3_), channel_id=1, source_target_pairs={{0,12},{4,8},{8,4},{12,0},{16,28},{20,24},{24,20},{28,16},{1,13},{... | collective-permute-start | bytes 196616 | tf_op jit(solution)/shard_map/ppermute | solution.py:53
  86.2 2.3 %collective-permute-done.26.refs_1_ = bf16[2,32,512]{2,1,0:T(8,128)(2,1)S(1)} collective-permute-done((bf16[2,32,512]{2,1,0:T(8,128)(2,1)S(1)}, bf16[2,32,512]{2,1,0:T(8,128)(2,1)S(1)}, u32[]{:S(2)}, u32[]{:S(2)}) %collective-permute-start.26) | collective-permute-done | bytes 65568 | tf_op jit(solution)/shard_map/ppermute | solution.py:53
  90.6 1.5 %collective-permute-start.32 = (bf16[256,512]{1,0:T(8,128)(2,1)S(1)}, bf16[256,512]{1,0:T(8,128)(2,1)S(1)}, u32[]{:S(2)}, u32[]{:S(2)}) collective-permute-start(bf16[256,512]{1,0:T(8,128)(2,1)S(1)} %bitcast.10), channel_id=1, source_target_pairs={{0,2},{1,3},{2,0},{3,1},{4,6},{5,7},{6,4},{7,5},{8,10},{9,11},{10,... | collective-permute-start | bytes 786440 | tf_op jit(solution)/shard_map/ppermute | solution.py:53
  92.1 1.8 %node_grads.1 = (bf16[256,1024]{1,0:T(8,128)(2,1)}, f32[1,512]{1,0:T(1,128)}) custom-call(s32[2]{0:T(128)S(1)} %pad_add_fusion.ids, bf16[1024,512]{1,0:T(8,128)(2,1)S(1)} %copy-done.2, bf16[272,128]{1,0:T(8,128)(2,1)S(1)} %get-tuple-element.149.refs_0_, bf16[272,128]{1,0:T(8,128)(2,1)S(1)} %collective-permute-done.29.refs_1_, ...), custom_call_target="tpu_custom_call" | custom-call | flops 268435456 | bytes 1835008 | tf_op jit(solution)/shard_map/node_grads/pallas_call | solution.py:588
  93.9 1.6 %place_weight.3.refs_1_ = f32[1024,512]{1,0:T(8,128)} custom-call(s32[2]{0:T(128)S(1)} %pad_add_fusion.ids, bf16[256,512]{1,0:T(8,128)(2,1)S(1)} %bitcast.11, bf16[256,512]{1,0:T(8,128)(2,1)S(1)} %collective-permute-done.33.refs_1_), custom_call_target="tpu_custom_call" | custom-call | bytes 1572864 | tf_op jit(solution)/shard_map/place_weight/pallas_call | solution.py:607
  95.5 3.8 %collective-permute-done.32.refs_0_ = bf16[256,512]{1,0:T(8,128)(2,1)S(1)} collective-permute-done((bf16[256,512]{1,0:T(8,128)(2,1)S(1)}, bf16[256,512]{1,0:T(8,128)(2,1)S(1)}, u32[]{:S(2)}, u32[]{:S(2)}) %collective-permute-start.32) | collective-permute-done | bytes 262176 | tf_op jit(solution)/shard_map/ppermute | solution.py:53
  (88 shorter events, 31.9 us)
Async XLA Ops:
  2.4 9.2 %collective-permute-start = (bf16[256,256]{1,0:T(8,128)(2,1)S(1)}, bf16[256,256]{1,0:T(8,128)(2,1)S(1)}, u32[]{:S(2)}, u32[]{:S(2)}) collective-permute-start(bf16[256,256]{1,0:T(8,128)(2,1)S(1)} %get-tuple-element.81), channel_id=1, source_target_pairs={{0,3},{1,2},{2,1},{3,0},{4,7},{5,6},{6,5},{7,4},{8,11},{9,10},{10,... | collective-permute-start | bytes 393224 | tf_op jit(solution)/shard_map/ppermute | solution.py:53
  4.9 6.9 %collective-permute-start.1 = (bf16[256,256]{1,0:T(8,128)(2,1)S(1)}, bf16[256,256]{1,0:T(8,128)(2,1)S(1)}, u32[]{:S(2)}, u32[]{:S(2)}) collective-permute-start(bf16[256,256]{1,0:T(8,128)(2,1)S(1)} %get-tuple-element.82), channel_id=1, source_target_pairs={{0,2},{1,3},{2,0},{3,1},{4,6},{5,7},{6,4},{7,5},{8,10},{9,11},{10,... | collective-permute-start | bytes 393224 | tf_op jit(solution)/shard_map/ppermute | solution.py:53
  5.5 6.2 %collective-permute-start.2 = (bf16[256,256]{1,0:T(8,128)(2,1)S(1)}, bf16[256,256]{1,0:T(8,128)(2,1)S(1)}, u32[]{:S(2)}, u32[]{:S(2)}) collective-permute-start(bf16[256,256]{1,0:T(8,128)(2,1)S(1)} %get-tuple-element.83), channel_id=1, source_target_pairs={{0,1},{1,0},{2,3},{3,2},{4,5},{5,4},{6,7},{7,6},{8,9},{9,8},{10,11... | collective-permute-start | bytes 393224 | tf_op jit(solution)/shard_map/ppermute | solution.py:53
  12.4 15.7 %collective-permute-start.3 = (bf16[4,128,256]{2,1,0:T(8,128)(2,1)S(1)}, bf16[4,128,256]{2,1,0:T(8,128)(2,1)S(1)}, u32[]{:S(2)}, u32[]{:S(2)}) collective-permute-start(bf16[4,128,256]{2,1,0:T(8,128)(2,1)S(1)} %get-tuple-element.85), channel_id=1, source_target_pairs={{0,16},{4,20},{8,24},{12,28},{16,0},{20,4},{24,8},{28,12},{1,17},{... | collective-permute-start | bytes 786440 | tf_op jit(solution)/shard_map/ppermute | solution.py:53
  15.9 15.0 %collective-permute-start.7 = (bf16[256,256]{1,0:T(8,128)(2,1)S(1)}, bf16[256,256]{1,0:T(8,128)(2,1)S(1)}, u32[]{:S(2)}, u32[]{:S(2)}) collective-permute-start(bf16[256,256]{1,0:T(8,128)(2,1)S(1)} %get-tuple-element.92), channel_id=1, source_target_pairs={{0,4},{4,0},{8,12},{12,8},{16,20},{20,16},{24,28},{28,24},{1,5},{5... | collective-permute-start | bytes 393224 | tf_op jit(solution)/shard_map/ppermute | solution.py:53
  17.3 15.0 %collective-permute-start.8 = (bf16[256,256]{1,0:T(8,128)(2,1)S(1)}, bf16[256,256]{1,0:T(8,128)(2,1)S(1)}, u32[]{:S(2)}, u32[]{:S(2)}) collective-permute-start(bf16[256,256]{1,0:T(8,128)(2,1)S(1)} %get-tuple-element.93), channel_id=1, source_target_pairs={{0,8},{4,12},{8,0},{12,4},{16,24},{20,28},{24,16},{28,20},{1,9},{5... | collective-permute-start | bytes 393224 | tf_op jit(solution)/shard_map/ppermute | solution.py:53
  18.9 13.4 %collective-permute-start.9 = (bf16[256,256]{1,0:T(8,128)(2,1)S(1)}, bf16[256,256]{1,0:T(8,128)(2,1)S(1)}, u32[]{:S(2)}, u32[]{:S(2)}) collective-permute-start(bf16[256,256]{1,0:T(8,128)(2,1)S(1)} %get-tuple-element.94), channel_id=1, source_target_pairs={{0,12},{4,8},{8,4},{12,0},{16,28},{20,24},{24,20},{28,16},{1,13},{... | collective-permute-start | bytes 393224 | tf_op jit(solution)/shard_map/ppermute | solution.py:53
  28.7 5.4 %collective-permute-start.4 = (bf16[256,256]{1,0:T(8,128)(2,1)S(1)}, bf16[256,256]{1,0:T(8,128)(2,1)S(1)}, u32[]{:S(2)}, u32[]{:S(2)}) collective-permute-start(bf16[256,256]{1,0:T(8,128)(2,1)S(1)} %get-tuple-element.88), channel_id=1, source_target_pairs={{0,4},{4,0},{8,12},{12,8},{16,20},{20,16},{24,28},{28,24},{1,5},{5... | collective-permute-start | bytes 393224 | tf_op jit(solution)/shard_map/ppermute | solution.py:53
  30.3 5.7 %collective-permute-start.5 = (bf16[256,256]{1,0:T(8,128)(2,1)S(1)}, bf16[256,256]{1,0:T(8,128)(2,1)S(1)}, u32[]{:S(2)}, u32[]{:S(2)}) collective-permute-start(bf16[256,256]{1,0:T(8,128)(2,1)S(1)} %get-tuple-element.89), channel_id=1, source_target_pairs={{0,8},{4,12},{8,0},{12,4},{16,24},{20,28},{24,16},{28,20},{1,9},{5... | collective-permute-start | bytes 393224 | tf_op jit(solution)/shard_map/ppermute | solution.py:53
  30.9 7.1 %collective-permute-start.6 = (bf16[256,256]{1,0:T(8,128)(2,1)S(1)}, bf16[256,256]{1,0:T(8,128)(2,1)S(1)}, u32[]{:S(2)}, u32[]{:S(2)}) collective-permute-start(bf16[256,256]{1,0:T(8,128)(2,1)S(1)} %get-tuple-element.90), channel_id=1, source_target_pairs={{0,12},{4,8},{8,4},{12,0},{16,28},{20,24},{24,20},{28,16},{1,13},{... | collective-permute-start | bytes 393224 | tf_op jit(solution)/shard_map/ppermute | solution.py:53
  39.5 6.4 %collective-permute-start.11 = (bf16[256,256]{1,0:T(8,128)(2,1)S(1)}, bf16[256,256]{1,0:T(8,128)(2,1)S(1)}, u32[]{:S(2)}, u32[]{:S(2)}) collective-permute-start(bf16[256,256]{1,0:T(8,128)(2,1)S(1)} %get-tuple-element.101), channel_id=1, source_target_pairs={{0,2},{1,3},{2,0},{3,1},{4,6},{5,7},{6,4},{7,5},{8,10},{9,11},{10,... | collective-permute-start | bytes 393224 | tf_op jit(solution)/shard_map/ppermute | solution.py:53
  41.2 6.6 %collective-permute-start.12 = (bf16[256,256]{1,0:T(8,128)(2,1)S(1)}, bf16[256,256]{1,0:T(8,128)(2,1)S(1)}, u32[]{:S(2)}, u32[]{:S(2)}) collective-permute-start(bf16[256,256]{1,0:T(8,128)(2,1)S(1)} %get-tuple-element.102), channel_id=1, source_target_pairs={{0,3},{1,2},{2,1},{3,0},{4,7},{5,6},{6,5},{7,4},{8,11},{9,10},{10,... | collective-permute-start | bytes 393224 | tf_op jit(solution)/shard_map/ppermute | solution.py:53
  49.3 6.4 %collective-permute-start.13 = (bf16[2,256,512]{2,1,0:T(8,128)(2,1)S(1)}, bf16[2,256,512]{2,1,0:T(8,128)(2,1)S(1)}, u32[]{:S(2)}, u32[]{:S(2)}) collective-permute-start(bf16[2,256,512]{2,1,0:T(8,128)(2,1)S(1)} %get-tuple-element.104), channel_id=1, source_target_pairs={{0,1},{1,0},{2,3},{3,2},{4,5},{5,4},{6,7},{7,6},{8,9},{9,8},{10,11... | collective-permute-start | bytes 1572872 | tf_op jit(solution)/shard_map/ppermute | solution.py:53
  49.9 4.3 %collective-permute-start.15 = (bf16[256,128]{1,0:T(8,128)(2,1)S(1)}, bf16[256,128]{1,0:T(8,128)(2,1)S(1)}, u32[]{:S(2)}, u32[]{:S(2)}) collective-permute-start(bf16[256,128]{1,0:T(8,128)(2,1)S(1)} %get-tuple-element.107), channel_id=1, source_target_pairs={{0,2},{1,3},{2,0},{3,1},{4,6},{5,7},{6,4},{7,5},{8,10},{9,11},{10,... | collective-permute-start | bytes 196616 | tf_op jit(solution)/shard_map/ppermute | solution.py:53
  51.5 4.2 %collective-permute-start.16 = (bf16[256,128]{1,0:T(8,128)(2,1)S(1)}, bf16[256,128]{1,0:T(8,128)(2,1)S(1)}, u32[]{:S(2)}, u32[]{:S(2)}) collective-permute-start(bf16[256,128]{1,0:T(8,128)(2,1)S(1)} %get-tuple-element.108), channel_id=1, source_target_pairs={{0,3},{1,2},{2,1},{3,0},{4,7},{5,6},{6,5},{7,4},{8,11},{9,10},{10,... | collective-permute-start | bytes 196616 | tf_op jit(solution)/shard_map/ppermute | solution.py:53
  55.8 8.4 %collective-permute-start.17 = (bf16[1,256,512]{2,1,0:T(8,128)(2,1)S(1)}, bf16[1,256,512]{2,1,0:T(8,128)(2,1)S(1)}, u32[]{:S(2)}, u32[]{:S(2)}) collective-permute-start(bf16[1,256,512]{2,1,0:T(8,128)(2,1)S(1)} %get-tuple-element.114), channel_id=1, source_target_pairs={{0,2},{1,3},{2,0},{3,1},{4,6},{5,7},{6,4},{7,5},{8,10},{9,11},{10,... | collective-permute-start | bytes 786440 | tf_op jit(solution)/shard_map/ppermute | solution.py:53
  57.9 5.7 %collective-permute-start.18 = (bf16[528,128]{1,0:T(8,128)(2,1)S(1)}, bf16[528,128]{1,0:T(8,128)(2,1)S(1)}, u32[]{:S(2)}, u32[]{:S(2)}) collective-permute-start(bf16[528,128]{1,0:T(8,128)(2,1)S(1)} %get-tuple-element.120), channel_id=1, source_target_pairs={{0,4},{4,0},{8,12},{12,8},{16,20},{20,16},{24,28},{28,24},{1,5},{5... | collective-permute-start | bytes 405512 | tf_op jit(solution)/shard_map/ppermute | solution.py:53
  58.8 9.6 %collective-permute-start.22 = (bf16[528,128]{1,0:T(8,128)(2,1)S(1)}, bf16[528,128]{1,0:T(8,128)(2,1)S(1)}, u32[]{:S(2)}, u32[]{:S(2)}) collective-permute-start(bf16[528,128]{1,0:T(8,128)(2,1)S(1)} %get-tuple-element.129), channel_id=1, source_target_pairs={{0,8},{4,12},{8,0},{12,4},{16,24},{20,28},{24,16},{28,20},{1,9},{5... | collective-permute-start | bytes 405512 | tf_op jit(solution)/shard_map/ppermute | solution.py:53
  60.4 8.1 %collective-permute-start.23 = (bf16[528,128]{1,0:T(8,128)(2,1)S(1)}, bf16[528,128]{1,0:T(8,128)(2,1)S(1)}, u32[]{:S(2)}, u32[]{:S(2)}) collective-permute-start(bf16[528,128]{1,0:T(8,128)(2,1)S(1)} %get-tuple-element.130), channel_id=1, source_target_pairs={{0,12},{4,8},{8,4},{12,0},{16,28},{20,24},{24,20},{28,16},{1,13},{... | collective-permute-start | bytes 405512 | tf_op jit(solution)/shard_map/ppermute | solution.py:53
  64.9 6.6 %collective-permute-start.19 = (bf16[2,32,512]{2,1,0:T(8,128)(2,1)S(1)}, bf16[2,32,512]{2,1,0:T(8,128)(2,1)S(1)}, u32[]{:S(2)}, u32[]{:S(2)}) collective-permute-start(bf16[2,32,512]{2,1,0:T(8,128)(2,1)S(1)} %get-tuple-element.123), channel_id=1, source_target_pairs={{0,4},{4,0},{8,12},{12,8},{16,20},{20,16},{24,28},{28,24},{1,5},{5... | collective-permute-start | bytes 196616 | tf_op jit(solution)/shard_map/ppermute | solution.py:53
  65.8 5.7 %collective-permute-start.20 = (bf16[2,32,512]{2,1,0:T(8,128)(2,1)S(1)}, bf16[2,32,512]{2,1,0:T(8,128)(2,1)S(1)}, u32[]{:S(2)}, u32[]{:S(2)}) collective-permute-start(bf16[2,32,512]{2,1,0:T(8,128)(2,1)S(1)} %get-tuple-element.124), channel_id=1, source_target_pairs={{0,8},{4,12},{8,0},{12,4},{16,24},{20,28},{24,16},{28,20},{1,9},{5... | collective-permute-start | bytes 196616 | tf_op jit(solution)/shard_map/ppermute | solution.py:53
  67.3 6.3 %collective-permute-start.21 = (bf16[2,32,512]{2,1,0:T(8,128)(2,1)S(1)}, bf16[2,32,512]{2,1,0:T(8,128)(2,1)S(1)}, u32[]{:S(2)}, u32[]{:S(2)}) collective-permute-start(bf16[2,32,512]{2,1,0:T(8,128)(2,1)S(1)} %get-tuple-element.125), channel_id=1, source_target_pairs={{0,12},{4,8},{8,4},{12,0},{16,28},{20,24},{24,20},{28,16},{1,13},{... | collective-permute-start | bytes 196616 | tf_op jit(solution)/shard_map/ppermute | solution.py:53
  69.1 11.8 %collective-permute-start.28 = (bf16[528,128]{1,0:T(8,128)(2,1)S(1)}, bf16[528,128]{1,0:T(8,128)(2,1)S(1)}, u32[]{:S(2)}, u32[]{:S(2)}) collective-permute-start(bf16[528,128]{1,0:T(8,128)(2,1)S(1)} %sum_mirror.1), channel_id=1, source_target_pairs={{0,16},{4,20},{8,24},{12,28},{16,0},{20,4},{24,8},{28,12},{1,17},{... | collective-permute-start | bytes 405512 | tf_op jit(solution)/shard_map/ppermute | solution.py:53
  73.6 6.3 %collective-permute-start.24 = (bf16[2,32,512]{2,1,0:T(8,128)(2,1)S(1)}, bf16[2,32,512]{2,1,0:T(8,128)(2,1)S(1)}, u32[]{:S(2)}, u32[]{:S(2)}) collective-permute-start(bf16[2,32,512]{2,1,0:T(8,128)(2,1)S(1)} %sum_half.1.here), channel_id=1, source_target_pairs={{0,16},{4,20},{8,24},{12,28},{16,0},{20,4},{24,8},{28,12},{1,17},{... | collective-permute-start | bytes 196616 | tf_op jit(solution)/shard_map/ppermute | solution.py:53
  79.9 4.3 %collective-permute-start.25 = (bf16[2,32,512]{2,1,0:T(8,128)(2,1)S(1)}, bf16[2,32,512]{2,1,0:T(8,128)(2,1)S(1)}, u32[]{:S(2)}, u32[]{:S(2)}) collective-permute-start(bf16[2,32,512]{2,1,0:T(8,128)(2,1)S(1)} %sum_both.1.refs_3_), channel_id=1, source_target_pairs={{0,4},{4,0},{8,12},{12,8},{16,20},{20,16},{24,28},{28,24},{1,5},{5... | collective-permute-start | bytes 196616 | tf_op jit(solution)/shard_map/ppermute | solution.py:53
  81.6 8.3 %collective-permute-start.29 = (bf16[272,128]{1,0:T(8,128)(2,1)S(1)}, bf16[272,128]{1,0:T(8,128)(2,1)S(1)}, u32[]{:S(2)}, u32[]{:S(2)}) collective-permute-start(bf16[272,128]{1,0:T(8,128)(2,1)S(1)} %get-tuple-element.142), channel_id=1, source_target_pairs={{0,1},{1,0},{2,3},{3,2},{4,5},{5,4},{6,7},{7,6},{8,9},{9,8},{10,11... | collective-permute-start | bytes 208904 | tf_op jit(solution)/shard_map/ppermute | solution.py:53
  81.7 8.2 %collective-permute-start.30 = (bf16[272,128]{1,0:T(8,128)(2,1)S(1)}, bf16[272,128]{1,0:T(8,128)(2,1)S(1)}, u32[]{:S(2)}, u32[]{:S(2)}) collective-permute-start(bf16[272,128]{1,0:T(8,128)(2,1)S(1)} %get-tuple-element.143), channel_id=1, source_target_pairs={{0,2},{1,3},{2,0},{3,1},{4,6},{5,7},{6,4},{7,5},{8,10},{9,11},{10,... | collective-permute-start | bytes 208904 | tf_op jit(solution)/shard_map/ppermute | solution.py:53
  83.2 6.7 %collective-permute-start.31 = (bf16[272,128]{1,0:T(8,128)(2,1)S(1)}, bf16[272,128]{1,0:T(8,128)(2,1)S(1)}, u32[]{:S(2)}, u32[]{:S(2)}) collective-permute-start(bf16[272,128]{1,0:T(8,128)(2,1)S(1)} %get-tuple-element.144), channel_id=1, source_target_pairs={{0,3},{1,2},{2,1},{3,0},{4,7},{5,6},{6,5},{7,4},{8,11},{9,10},{10,... | collective-permute-start | bytes 208904 | tf_op jit(solution)/shard_map/ppermute | solution.py:53
  83.6 4.9 %collective-permute-start.26 = (bf16[2,32,512]{2,1,0:T(8,128)(2,1)S(1)}, bf16[2,32,512]{2,1,0:T(8,128)(2,1)S(1)}, u32[]{:S(2)}, u32[]{:S(2)}) collective-permute-start(bf16[2,32,512]{2,1,0:T(8,128)(2,1)S(1)} %sum_both.1.refs_3_), channel_id=1, source_target_pairs={{0,8},{4,12},{8,0},{12,4},{16,24},{20,28},{24,16},{28,20},{1,9},{5... | collective-permute-start | bytes 196616 | tf_op jit(solution)/shard_map/ppermute | solution.py:53
  84.2 5.7 %collective-permute-start.27 = (bf16[2,32,512]{2,1,0:T(8,128)(2,1)S(1)}, bf16[2,32,512]{2,1,0:T(8,128)(2,1)S(1)}, u32[]{:S(2)}, u32[]{:S(2)}) collective-permute-start(bf16[2,32,512]{2,1,0:T(8,128)(2,1)S(1)} %sum_both.1.refs_3_), channel_id=1, source_target_pairs={{0,12},{4,8},{8,4},{12,0},{16,28},{20,24},{24,20},{28,16},{1,13},{... | collective-permute-start | bytes 196616 | tf_op jit(solution)/shard_map/ppermute | solution.py:53
  90.5 3.4 %collective-permute-start.33 = (bf16[256,512]{1,0:T(8,128)(2,1)S(1)}, bf16[256,512]{1,0:T(8,128)(2,1)S(1)}, u32[]{:S(2)}, u32[]{:S(2)}) collective-permute-start(bf16[256,512]{1,0:T(8,128)(2,1)S(1)} %bitcast.9), channel_id=1, source_target_pairs={{0,1},{1,0},{2,3},{3,2},{4,5},{5,4},{6,7},{7,6},{8,9},{9,8},{10,11... | collective-permute-start | bytes 786440 | tf_op jit(solution)/shard_map/ppermute | solution.py:53
  90.6 8.7 %collective-permute-start.32 = (bf16[256,512]{1,0:T(8,128)(2,1)S(1)}, bf16[256,512]{1,0:T(8,128)(2,1)S(1)}, u32[]{:S(2)}, u32[]{:S(2)}) collective-permute-start(bf16[256,512]{1,0:T(8,128)(2,1)S(1)} %bitcast.10), channel_id=1, source_target_pairs={{0,2},{1,3},{2,0},{3,1},{4,6},{5,7},{6,4},{7,5},{8,10},{9,11},{10,... | collective-permute-start | bytes 786440 | tf_op jit(solution)/shard_map/ppermute | solution.py:53
  (9 other events, 70.9 us)
